TPU v7x, 128 devices: a whole 4x4x4 slice. The times are simulated.
128 devices in a mesh: lat: 4 (over z_lo, core), lon: 32 (over z_hi, x, y).
Axes of the slice: x: 4, y: 4, z: 4 (z_hi: 2, z_lo: 2; z = z_hi * 2 + z_lo), core: 2. Of those that a mesh axis runs over, the one named last changes fastest.
Arguments:
- tokens: bfloat16 [2, 72, 768, 1024], P(None, 'lat', 'lon'), may hold values from -6 to 6
- norm_gain: float32 [1024], replicated, may hold values from 0.1 to 1.9
- attention_in: bfloat16 [1024, 3072], replicated, may hold values from -0.1875 to 0.1875
- attention_out: bfloat16 [1024, 1024], replicated, may hold values from -0.1875 to 0.1875
- head_bias: float32 [16, 144, 144], replicated, may hold values from -3 to 400
- cotangent: bfloat16 [2, 72, 768, 1024], P(None, 'lat', 'lon'), may hold values from -6 to 6
Outputs:
- output: bfloat16 [2, 72, 768, 1024], P(None, 'lat', 'lon')
- grad_tokens: bfloat16 [2, 72, 768, 1024], P(None, 'lat', 'lon')
- grad_in: bfloat16 [1024, 3072], P(('lat', 'lon'))
- grad_out: bfloat16 [1024, 1024], P(('lat', 'lon'))
- grad_gain: float32 [1024], P(('lat', 'lon'))
All inputs are finite; a program needn't handle non-finite values.
Results may differ from a plain program's by a relative error of at most 0.014.
Values may be sent and summed in bfloat16 or wider, within the bound.
A program may use at most 192 MiB of HBM per device.

v0:
```python
import math

import jax
import jax.numpy as jnp
from jax import lax
from jax.sharding import PartitionSpec as P

LEV = 2
WIN_LAT = 6
WIN_LON = 12
SH = 3
SW = 6


def passed_along(block, axis, distance):
    devices = range(lax.axis_size(axis))
    route = [((i - distance) % len(devices), i) for i in devices]
    return lax.ppermute(block, axis, route)


def layer_stats(tokens):
    values = tokens.astype(jnp.float32)
    average = jnp.mean(values, axis=-1, keepdims=True)
    centred = values - average
    variance = jnp.mean(centred * centred, axis=-1, keepdims=True)
    inverse = lax.rsqrt(variance + 1e-05)
    return (centred * inverse, inverse)


def norm_back(cotangent, grad_normed, standard, inverse, norm_gain):
    grad_float = grad_normed.astype(jnp.float32)
    grad_gain = jnp.sum(grad_float * standard, axis=(0, 1, 2))
    grad_scaled = grad_float * norm_gain
    first = jnp.mean(grad_scaled, axis=-1, keepdims=True)
    second = jnp.mean(grad_scaled * standard, axis=-1, keepdims=True)
    grad_local = inverse * (grad_scaled - first - standard * second)
    return ((cotangent.astype(jnp.float32) + grad_local).astype(jnp.bfloat16), grad_gain)


def region_grid(lat_rows, nlat, breadth):
    labels = (lat_rows >= nlat - 2 * SH).astype(jnp.int32) + (lat_rows >= nlat - SH).astype(
        jnp.int32
    )
    return jnp.broadcast_to(labels[None, :, None, None], (LEV, lat_rows.shape[0], breadth, 1))


def to_windows(grid):
    levels, height, breadth, depth = grid.shape
    shaped = grid.reshape(levels, height // WIN_LAT, WIN_LAT, breadth // WIN_LON, WIN_LON, depth)
    return shaped.transpose(1, 3, 0, 2, 4, 5).reshape(-1, levels * WIN_LAT * WIN_LON, depth)


def from_windows(blocks, height, breadth):
    depth = blocks.shape[-1]
    shaped = blocks.reshape(height // WIN_LAT, breadth // WIN_LON, LEV, WIN_LAT, WIN_LON, depth)
    return shaped.transpose(2, 0, 3, 1, 4, 5).reshape(LEV, height, breadth, depth)


def attend(shifted, grad_back, region, attention_in, attention_out, head_bias):
    blocks, window, width = shifted.shape
    head_count = head_bias.shape[0]
    head_size = width // head_count
    scaling = 1.0 / math.sqrt(head_size)
    token_rows = shifted.reshape(blocks * window, width)
    projected = jnp.dot(token_rows, attention_in, preferred_element_type=jnp.float32).astype(
        jnp.bfloat16
    )
    projected = projected.reshape(blocks, window, 3, head_count, head_size)
    query_part = projected[:, :, 0]
    key_part = projected[:, :, 1]
    value_part = projected[:, :, 2]
    scores = (
        jnp.einsum("bqhe,bkhe->bhqk", query_part, key_part, preferred_element_type=jnp.float32)
        * scaling
        + head_bias[None]
    )
    allowed = (region[:, :, None] == region[:, None, :])[:, None]
    scores = jnp.where(allowed, scores, -1000000000.0)
    highest = jnp.max(scores, axis=-1, keepdims=True)
    powers = jnp.exp(scores - highest)
    weights = powers / jnp.sum(powers, axis=-1, keepdims=True)
    weights_b = weights.astype(jnp.bfloat16)
    context = jnp.einsum(
        "bhqk,bkhe->bqhe", weights_b, value_part, preferred_element_type=jnp.float32
    ).astype(jnp.bfloat16)
    context = context.reshape(blocks * window, width)
    attended = jnp.dot(context, attention_out, preferred_element_type=jnp.float32).astype(
        jnp.bfloat16
    )
    flat_grad = grad_back.reshape(blocks * window, width)
    grad_context = jnp.einsum(
        "re,de->rd", flat_grad, attention_out, preferred_element_type=jnp.float32
    ).astype(jnp.bfloat16)
    grad_out = jnp.einsum("rd,re->de", context, flat_grad, preferred_element_type=jnp.float32)
    grad_context = grad_context.reshape(blocks, window, head_count, head_size)
    grad_weights = jnp.einsum(
        "bqhe,bkhe->bhqk", grad_context, value_part, preferred_element_type=jnp.float32
    )
    grad_value = jnp.einsum(
        "bhqk,bqhe->bkhe", weights_b, grad_context, preferred_element_type=jnp.float32
    ).astype(jnp.bfloat16)
    inner = jnp.sum(grad_weights * weights, axis=-1, keepdims=True)
    grad_scores = (weights * (grad_weights - inner)).astype(jnp.bfloat16)
    grad_query = (
        jnp.einsum("bhqk,bkhe->bqhe", grad_scores, key_part, preferred_element_type=jnp.float32)
        * scaling
    ).astype(jnp.bfloat16)
    grad_key = (
        jnp.einsum("bhqk,bqhe->bkhe", grad_scores, query_part, preferred_element_type=jnp.float32)
        * scaling
    ).astype(jnp.bfloat16)
    grad_projected = jnp.stack([grad_query, grad_key, grad_value], axis=2).reshape(
        blocks * window, 3 * width
    )
    grad_rows = jnp.einsum(
        "rc,dc->rd", grad_projected, attention_in, preferred_element_type=jnp.float32
    ).astype(jnp.bfloat16)
    grad_in = jnp.einsum(
        "rd,rc->dc", token_rows, grad_projected, preferred_element_type=jnp.float32
    )
    return (
        attended.reshape(blocks, window, width),
        grad_rows.reshape(blocks, window, width),
        grad_in,
        grad_out,
    )


def move_ahead(fields, lat_move, lon_move):
    strips = lat_move(jnp.stack([field[:, :SH] for field in fields]))
    fields = [
        jnp.concatenate([field[:, SH:], strips[place]], 1) for place, field in enumerate(fields)
    ]
    strips = lon_move(jnp.stack([field[:, :, :SW] for field in fields]))
    return [
        jnp.concatenate([field[:, :, SW:], strips[place]], 2) for place, field in enumerate(fields)
    ]


def move_behind(fields):
    strips = passed_along(jnp.stack([field[:, -SH:] for field in fields]), "lat", 1)
    fields = [
        jnp.concatenate([strips[place], field[:, :-SH]], 1) for place, field in enumerate(fields)
    ]
    strips = passed_along(jnp.stack([field[:, :, -SW:] for field in fields]), "lon", 1)
    return [
        jnp.concatenate([strips[place], field[:, :, :-SW]], 2) for place, field in enumerate(fields)
    ]


def local(tokens, norm_gain, attention_in, attention_out, head_bias, cotangent):
    height = tokens.shape[1]
    breadth = tokens.shape[2]
    width = tokens.shape[3]
    standard, inverse = layer_stats(tokens)
    normed = (standard * norm_gain).astype(jnp.bfloat16)

    def lat_move(strip):
        return passed_along(strip, "lat", -1)

    def lon_move(strip):
        return passed_along(strip, "lon", -1)

    shifted = move_ahead([normed], lat_move, lon_move)[0]
    grad_shifted = move_ahead([cotangent], lat_move, lon_move)[0]
    lat_rows = lax.axis_index("lat") * height + jnp.arange(height, dtype=jnp.int32)
    region = region_grid(lat_rows, height * lax.axis_size("lat"), breadth)
    shifted_win = to_windows(shifted)
    grad_win = to_windows(grad_shifted)
    region_win = to_windows(region)[..., 0]
    total = shifted_win.shape[0]
    batch = math.gcd(total, 4)
    turns = total // batch
    window = shifted_win.shape[1]

    def one_batch(carry, item):
        attended, grad_rows, grad_in, grad_out = attend(
            item[0], item[1], item[2], attention_in, attention_out, head_bias
        )
        return ((carry[0] + grad_in, carry[1] + grad_out), (attended, grad_rows))

    start = (jnp.zeros((width, 3 * width), jnp.float32), jnp.zeros((width, width), jnp.float32))
    items = (
        shifted_win.reshape(turns, batch, window, width),
        grad_win.reshape(turns, batch, window, width),
        region_win.reshape(turns, batch, window),
    )
    sums, outs = lax.scan(one_batch, start, items)
    attended = from_windows(outs[0].reshape(total, window, width), height, breadth)
    grad_rows = from_windows(outs[1].reshape(total, window, width), height, breadth)
    back_attn, grad_normed = move_behind([attended, grad_rows])
    output = (tokens.astype(jnp.float32) + back_attn.astype(jnp.float32)).astype(jnp.bfloat16)
    grad_tokens, gain_term = norm_back(cotangent, grad_normed, standard, inverse, norm_gain)
    totals = (
        lax.psum_scatter(sums[0], ("lat", "lon"), scatter_dimension=0, tiled=True),
        lax.psum_scatter(sums[1], ("lat", "lon"), scatter_dimension=0, tiled=True),
        lax.psum_scatter(gain_term, ("lat", "lon"), scatter_dimension=0, tiled=True),
    )
    return (
        output,
        grad_tokens,
        totals[0].astype(jnp.bfloat16),
        totals[1].astype(jnp.bfloat16),
        totals[2],
    )


def solution(mesh):
    placed = (P(None, "lat", "lon", None), P(), P(), P(), P(), P(None, "lat", "lon", None))
    return jax.shard_map(
        local,
        mesh=mesh,
        in_specs=placed,
        out_specs=(
            P(None, "lat", "lon", None),
            P(None, "lat", "lon", None),
            P(("lat", "lon"), None),
            P(("lat", "lon"), None),
            P(("lat", "lon")),
        ),
        check_vma=False,
    )
```

profile of v0, /device:TPU:96, one launch (start us, length us, event | category | flops | bytes accessed | tf_op | source)
XLA Modules:
  0.0 1794.4 jit_solution(4013693765892957765)
XLA Ops:
  7.2 3.3 convert_reduce_fusion
  10.5 3.0 fusion.27
  13.7 3.5 multiply_convert_fusion.3
  23.9 3.5 copy.67
  29.5 5.3 collective-permute-start.1
  39.8 5.6 collective-permute-done.1
  45.4 2.3 pad_maximum_fusion.3
  49.5 4.7 collective-permute-done.3
  54.2 2.3 pad_maximum_fusion.4
  56.5 3.2 copy.65
  59.7 271.9 %while.17 = (s32[]{:T(128)}, f32[1024,3072]{1,0:T(8,128)}, f32[1024,1024]{1,0:T(8,128)}, bf16[3,2,144,1024]{3,1,2,0:T(2,128)(2,1)}, bf16[3,2,144,1024]{3,1,2,0:T...) while((s32[]{:T(128)}, f32[1024,3072]{1,0:T(8,128)}, ...), condition=%wide.region_6.7_spmd.clone, body=%wide.region_2.6_spmd.clone.sunk | while | flops 7783706624 | bytes 200789456 | solution.py:188
  76.8 6.0 convolution_convert_fusion.11
  82.9 4.3 reshape.106
  89.3 2.1 copy.112
  94.2 3.0 fusion.117
  99.0 4.2 fusion.121
  106.9 3.4 convolution_convert_fusion.13
  118.3 4.1 multiply_reduce_fusion.2
  122.4 3.6 multiply_convert_fusion.5
  128.6 2.3 pad_maximum_fusion.10
  131.0 5.3 copy.115
  136.3 3.4 reshape.107
  139.8 5.4 convolution_convert_fusion.12
  145.2 2.2 copy_dynamic-update-slice_fusion.3
  147.4 3.3 select_add_fusion.5
  150.7 6.4 select_add_fusion.4
  158.7 6.0 convolution_convert_fusion.11
  164.7 4.3 reshape.106
  171.1 2.1 copy.112
  176.0 3.0 fusion.117
  180.8 4.2 fusion.121
  188.7 3.4 convolution_convert_fusion.13
  200.1 4.1 multiply_reduce_fusion.2
  204.2 3.6 multiply_convert_fusion.5
  210.4 2.3 pad_maximum_fusion.10
  212.8 5.3 copy.115
  218.1 3.4 reshape.107
  221.6 5.4 convolution_convert_fusion.12
  227.0 2.2 copy_dynamic-update-slice_fusion.3
  229.2 5.6 select_add_fusion.5
  234.9 9.3 select_add_fusion.4
  245.7 6.0 convolution_convert_fusion.11
  251.7 4.3 reshape.106
  263.0 3.0 fusion.117
  267.8 4.2 fusion.121
  275.7 3.4 convolution_convert_fusion.13
  287.1 4.1 multiply_reduce_fusion.2
  291.2 3.6 multiply_convert_fusion.5
  297.5 2.3 pad_maximum_fusion.10
  299.8 5.3 copy.115
  305.1 3.4 reshape.107
  308.6 5.4 convolution_convert_fusion.12
  314.0 2.2 copy_dynamic-update-slice_fusion.3
  316.3 5.6 select_add_fusion.5
  321.9 9.3 select_add_fusion.4
  335.0 2.2 copy.72
  341.3 6.5 collective-permute-done.4
  349.7 2.2 pad_maximum_fusion.5
  351.9 29.2 %collective-permute-done.5 = bf16[2,2,18,6,1024]{4,1,3,2,0:T(2,128)(2,1)} collective-permute-done((bf16[2,2,18,6,1024]{4,1,3,2,0:T(2,128)(2,1)}, bf16[2,2,18,6,1024]{4,1,3,2,0:T(2,128)(2,1)}, u32[]{:S(2)}, u32[]{:S(2)}) %collective-permute-start.5) | collective-permute-done | bytes 884768 | tf_op jit(solution)/shard_map/ppermute | solution.py:18
  382.9 12.9 fusion.32
  395.8 11.8 fusion.34
  411.1 63.9 %all-reduce = f32[1024]{0:T(1024)S(1)} all-reduce(f32[1024]{0:T(1024)S(1)} %get-tuple-element.148), channel_id=4, replica_groups=mesh['lat'=4,'lon'=32] {'lat','lon'}, use_global_device_ids=true, to_apply=%region_12.13.clone | all-reduce | flops 1024 | bytes 8192
  475.6 577.2 %reduce-scatter.5.cloned.1.call-done = f32[8,1024]{1,0:T(8,128)} async-done(((f32[1024,1024]{1,0:T(8,128)}), f32[8,1024]{1,0:T(8,128)}) %reduce-scatter.5.cloned.1.call-update) | async-done | bytes 32784 | tf_op jit(solution)/shard_map/reduce_scatter | solution.py:196
  1054.2 731.6 %reduce-scatter.3.cloned.1.call-done = f32[8,3072]{1,0:T(8,128)} async-done(((f32[1024,3072]{1,0:T(8,128)}), f32[8,3072]{1,0:T(8,128)}) %reduce-scatter.3.cloned.1.call-update) | async-done | bytes 98320 | tf_op jit(solution)/shard_map/reduce_scatter | solution.py:195
  (235 shorter events, 102.9 us)
Async XLA Ops:
  7.2 3.4 copy-start.8
  7.2 6.4 copy-start.28
  7.2 1045.6 %reduce-scatter.5.cloned.1.call-start = ((), (), s32[]{:S(2)}) async-start(), calls=%async_computation.3 | async-start | bytes 4227072 | tf_op jit(solution)/shard_map/reduce_scatter | solution.py:196
  10.5 6.6 copy-start.18
  13.6 4.4 copy-start.20
  13.6 4.4 copy-start.16
  18.1 10.9 collective-permute-start
  20.9 15.8 collective-permute-start.2
  29.5 15.9 collective-permute-start.1
  37.2 17.0 collective-permute-start.3
  75.4 1.2 copy-start.14
  89.3 2.1 copy-start.2
  92.5 1.7 copy-start.25
  94.2 3.0 copy-start.1
  110.3 2.6 copy-start.30
  118.3 9.1 slice-start
  122.4 5.0 slice-start.1
  126.5 1.2 copy-start.10
  139.8 5.4 copy-start.11
  145.2 2.3 copy-start.5
  145.2 2.3 copy-start.7
  147.4 3.3 copy-start
  147.4 3.3 copy-start.4
  150.7 6.4 copy-start.15
  157.2 1.2 copy-start.14
  171.1 2.1 copy-start.2
  174.3 1.7 copy-start.25
  176.0 3.0 copy-start.1
  192.1 2.6 copy-start.30
  200.1 9.1 slice-start
  204.2 5.0 slice-start.1
  221.6 5.4 copy-start.11
  227.0 2.3 copy-start.5
  227.0 2.3 copy-start.7
  229.2 5.6 copy-start
  229.2 5.6 copy-start.4
  234.9 9.3 copy-start.15
  244.2 1.2 copy-start.14
  258.1 2.1 copy-start.2
  261.4 1.7 copy-start.25
  263.0 3.0 copy-start.1
  279.1 2.6 copy-start.30
  287.1 9.1 slice-start
  291.2 5.0 slice-start.1
  295.3 1.2 copy-start.10
  308.6 5.4 copy-start.11
  314.0 2.3 copy-start.5
  314.0 2.3 copy-start.7
  316.3 5.6 copy-start
  316.3 5.6 copy-start.4
  321.9 9.3 copy-start.15
  331.6 1454.2 %reduce-scatter.3.cloned.1.call-start = ((), (), s32[]{:S(2)}) async-start(), calls=%async_computation.2 | async-start | bytes 12681216 | tf_op jit(solution)/shard_map/reduce_scatter | solution.py:195
  331.7 1.5 copy-start.26
  332.4 2.6 copy-start.27
  338.4 9.4 collective-permute-start.4
  341.3 8.3 copy-start.12
  349.1 33.7 %copy-start.9 = (bf16[2,18,24,1024]{3,2,1,0:T(8,128)(2,1)S(1)}, bf16[2,18,24,1024]{3,2,1,0:T(8,128)(2,1)}, u32[]{:S(2)}) copy-start(bf16[2,18,24,1024]{3,2,1,0:T(8,128)(2,1)} %param.8) | copy-start | bytes 5308420
  349.1 33.7 %copy-start.19 = (f32[2,18,24]{0,2,1:T(8,128)S(1)}, f32[2,18,24]{0,2,1:T(8,128)}, u32[]{:S(2)}) copy-start(f32[2,18,24]{0,2,1:T(8,128)} %copy-done.18) | copy-start | bytes 10372
  349.1 33.7 %copy-start.29 = (f32[1024]{0:T(1024)S(1)}, f32[1024]{0:T(1024)}, u32[]{:S(2)}) copy-start(f32[1024]{0:T(1024)} %param.9) | copy-start | bytes 12292
  351.9 29.2 %collective-permute-start.5 = (bf16[2,2,18,6,1024]{4,1,3,2,0:T(2,128)(2,1)}, bf16[2,2,18,6,1024]{4,1,3,2,0:T(2,128)(2,1)}, u32[]{:S(2)}, u32[]{:S(2)}) collective-permute-start(bf16[2,2,18,6,1024]{4,1,3,2,0:T(2,128)(2,1)} %pad_maximum_fusion.5), channel_id=1, source_target_pairs={{31,0},{0,1},{1,2},{2,3},{3,4},{4,5},{5,6},{6,7},{7,8},{8,9},{9,10... | collective-permute-start | bytes 2654216 | tf_op jit(solution)/shard_map/ppermute | solution.py:18
  351.9 31.0 %copy-start.13 = (bf16[2,15,24,1024]{3,0,2,1:T(2,128)(2,1)S(1)}, bf16[2,15,24,1024]{3,0,2,1:T(2,128)(2,1)}, u32[]{:S(2)}) copy-start(bf16[2,15,24,1024]{3,0,2,1:T(2,128)(2,1)} %copy-done.12) | copy-start | bytes 4423684
  382.8 13.0 copy-start.17
  382.8 13.0 copy-start.21
  382.8 13.0 copy-start.23
  (9 other events, 8.0 us)
Sparse Core Ops, SparseCore 0:
  331.7 721.0 reduce-scatter.4
  1055.3 730.4 reduce-scatter.2
where the time goes:
time: 1800 us; the launch traced here: 1790 us
  waiting for transfers between devices  1360 us (76%)
  local copies, waits for them, and re-layouts  136 us (8%)
  matrix products  123 us (7%)
  other arithmetic  77.9 us (4%)
  blocking collectives  63.9 us (4%)
    reduce_scatter x1, waiting for transfers between devices, local(): lax.psum_scatter(sums[0], ('lat', 'lon'), scatter_dimension=0, tiled=True)  732 us
    reduce_scatter x1, waiting for transfers between devices, local(): lax.psum_scatter(sums[1], ('lat', 'lon'), scatter_dimension=0, tiled=True)  577 us
    unnamed x1, blocking collectives  63.9 us
    ppermute x6, waiting for transfers between devices, passed_along(): return lax.ppermute(block, axis, route)  46 us
  transfers between devices with their start and end apart: 8, of which 6 were waited for; matrix products, arithmetic and copies ran while one was open for 3% of the time, Pallas kernels for 0%

commit v1 on v0

v1 whole, which is shorter than its diff:
```python
import jax
import jax.numpy as jnp
import numpy as np
from jax import lax
from jax.experimental import pallas as pl
from jax.experimental.pallas import tpu as pltpu
from jax.sharding import PartitionSpec as P

D = 1024
WINT = 144
PAIR = 288
OWN = 864
STRIP = 384
NT = (((1,), (1,)), ((), ()))
TN = (((0,), (0,)), ((), ()))
BF = jnp.bfloat16
F32 = jnp.float32

WINDOWS = ((0, 0), (1, 0), (2, 0), (2, 1), (0, 1), (1, 1))

AXES = ("x", "y", "z")
ORDERS = (("x", "y", "z"), ("y", "z", "x"), ("z", "x", "y"))
PIECES = (
    tuple((("in", 1024 * g, 512),) for g in range(3)),
    (
        (("in", 512, 512), ("out", 0, 512)),
        (("in", 1536, 512), ("out", 512, 256)),
        (("in", 2560, 512), ("out", 768, 256)),
    ),
)
LANES = tuple(tuple(sum(p[2] for p in group) // 2 for group in rnd) for rnd in PIECES)
FIRST = ((128, 128, 128), (256, 256, 128))
SIZES = {"zl": 2, "zh": 2, "x": 4, "y": 4}


def left_dims(dims, axis):
    gone = ("zl", "zh") if axis == "z" else (axis,)
    return tuple(d for d in dims if d not in gone)


def strip_cells():
    cells = [(l, r, c) for l in range(2) for r in range(3) for c in range(24)]
    cells += [(l, r, c) for l in range(2) for r in range(3, 15) for c in range(6)]
    cells += [(l, r, c) for l in range(2) for r in range(15, 18) for c in range(6)] + [None] * 12
    cells += [(l, r, c) for l in range(2) for r in range(3) for c in range(6)] + [None] * 12
    return cells


def window_cells():
    return [
        (l, 3 + 6 * i + a, 6 + 12 * j + b)
        for i, j in WINDOWS
        for l in range(2)
        for a in range(6)
        for b in range(12)
    ]


def received_cells():
    cells = []
    for n, cell in enumerate(strip_cells()):
        if cell is None:
            cells.append(None)
            continue
        l, r, c = cell
        if n < 144 or n >= 336:
            r += 18
        if n >= 144:
            c += 24
        cells.append((l, r, c))
    return cells


def one_hot(targets, sources):
    place = {}
    for n, cell in enumerate(sources):
        if cell is not None and cell not in place:
            place[cell] = n
    out = np.zeros((len(targets), len(sources)), np.float32)
    for n, cell in enumerate(targets):
        if cell is not None and cell in place:
            out[n, place[cell]] = 1
    return out


def permutations():
    own = [(l, r, c) for l in range(2) for r in range(18) for c in range(24)]
    strips = strip_cells()
    got = received_cells()
    win = window_cells()
    wide = own[64:368] + own[496:800]
    mid = own[72:360] + own[504:792]
    bottom = own[360:432] + own[792:864]
    top = own[:72] + own[432:504]
    return (
        one_hot(strips, own),
        one_hot(win[:288], wide),
        one_hot(win[288:576], own[352:432] + own[784:864] + got[:144] + got[288:]),
        one_hot(win[576:], wide + got[144:288]),
        one_hot(got[:144] + got[288:], win[288:576]),
        one_hot(got[144:288], win[576:]),
        one_hot(mid, win[:288] + win[576:] + strips[144:288]),
        one_hot(bottom, win[288:576] + strips[288:336]),
        one_hot(top, [c if c is not None and c[2] >= 6 else None for c in strips[:144]] + strips[336:]),
    )


def region_mask():
    region = np.array([a < 3 for l in range(2) for a in range(6) for b in range(12)])
    one = np.where(region[:, None] == region[None, :], 0.0, -1e9).astype(np.float32)
    return np.concatenate([one, one], 0)


def dg(a, b, dims):
    return lax.dot_general(a, b, dims, preferred_element_type=F32)


def dot(a, b):
    return jnp.dot(a, b, preferred_element_type=F32)


def mesh_place(core, x, y, z):
    return ((z % 2) * 2 + core, (z // 2) * 16 + x * 4 + y)


def block_kernel(
    tok_hbm, cot_hbm, gain_ref, win_hbm, wout_hbm, hb_hbm, mask_ref,
    pack_ref, p0_ref, p1_ref, p2_ref, r1_ref, r2_ref, imid_ref, ibot_ref, itop_ref,
    out_hbm, gt_hbm, gi_out, go_out, gg_out,
    *scratch,
):
    scratch = list(scratch)

    def take(count):
        out = scratch[:count]
        del scratch[:count]
        return out

    own_x, own_c, xw, cw, nw, nwt, ct, proj, gctx, win, wout, bias, mask = take(13)
    send_strip, recv_strip = take(4), take(4)
    sends = [take(3), take(3)]
    owns = [take(3), take(3)]
    halves = [take(3), take(3)]
    landing = {(r, g, p): take(8) for r in range(2) for g in range(3) for p in range(3)}
    middles = {(r, g, p): take(1)[0] for r in range(2) for g in range(3) for p in range(2)}
    gain_mine, gain_land = take(2)
    load_sem, strip_send, strip_recv, core_send, core_recv = take(5)
    ring_send, ring_recv, gain_send, gain_recv = take(4)

    lat = lax.axis_index("lat")
    lon = lax.axis_index("lon")
    core = lat % 2
    me = {"x": (lon // 4) % 4, "y": lon % 4, "z": (lon // 16) * 2 + lat // 2}

    def device(axis, step):
        at = dict(me)
        at[axis] = (me[axis] + step + 4) % 4
        return mesh_place(core, at["x"], at["y"], at["z"])

    sibling = mesh_place(1 - core, me["x"], me["y"], me["z"])

    def grid_place(a, b):
        return ((lat + a + 4) % 4, (lon + b + 32) % 32)

    loads = [
        pltpu.make_async_copy(src, dst, load_sem.at[n])
        for n, (src, dst) in enumerate(
            ((tok_hbm, own_x), (cot_hbm, own_c), (win_hbm, win), (wout_hbm, wout), (hb_hbm, bias))
        )
    ]
    for load in loads:
        load.start()

    barrier = pltpu.get_barrier_semaphore()
    partners = [sibling] + [device(a, s) for a in AXES for s in (1, -1)]
    partners += [grid_place(s * a, s * b) for a, b in ((1, 0), (0, 1), (1, 1)) for s in (1, -1)]
    for other in partners:
        pl.semaphore_signal(barrier, inc=1, device_id=other, device_id_type=pl.DeviceIdType.MESH)
    pl.semaphore_wait(barrier, len(partners))

    def remote(src, dst, send, recv, place):
        copy = pltpu.make_async_remote_copy(
            src_ref=src,
            dst_ref=dst,
            send_sem=send,
            recv_sem=recv,
            device_id=place,
            device_id_type=pl.DeviceIdType.MESH,
        )
        copy.start()
        return copy

    PARTS = ((0, 144, 1, 0), (144, 192, 0, 1), (336, 48, 1, 1))

    def send_strips(number, way, parts=(0, 1, 2)):
        copies = []
        for part in parts:
            low, size, a, b = PARTS[part]
            copies.append(
                remote(
                    send_strip[number].at[pl.ds(low, size)],
                    recv_strip[number].at[pl.ds(low, size)],
                    strip_send.at[number, part],
                    strip_recv.at[number, part],
                    grid_place(way * a, way * b),
                )
            )
        return copies

    strip_copies = []
    for number, own in ((0, own_x), (1, own_c)):
        loads[number].wait()
        send_strip[number][...] = dot(pack_ref[...], own[...]).astype(BF)
        strip_copies.append(send_strips(number, -1))

    def gathered(own, strip, s):
        if s == 1:
            parts = [own[352:432], own[784:864], strip[0:144], strip[288:384]]
            return dot(p1_ref[...], jnp.concatenate(parts, 0))
        parts = [own[64:368], own[496:800]]
        if s == 0:
            return dot(p0_ref[...], jnp.concatenate(parts, 0))
        return dot(p2_ref[...], jnp.concatenate(parts + [strip[144:288]], 0))

    def standardised(x):
        centred = x - jnp.mean(x, axis=-1, keepdims=True)
        inverse = lax.rsqrt(jnp.mean(centred * centred, axis=-1, keepdims=True) + 1e-5)
        return centred * inverse, inverse

    def gather_step(s):
        rows = slice(s * PAIR, (s + 1) * PAIR)
        x = gathered(own_x, recv_strip[0], s)
        xw[rows] = x.astype(BF)
        standard, _ = standardised(x)
        nw[rows] = (standard * gain_ref[...]).astype(BF)
        cw[rows] = gathered(own_c, recv_strip[1], s).astype(BF)

    def project(s, count):
        rows = slice(s * PAIR, s * PAIR + count)

        def columns(n, _):
            at = pl.ds(pl.multiple_of(n * 512, 512), 512)
            value = dot(nw[rows], win[:, at])
            proj[rows, at] = (value * jnp.where(n < 2, 0.125, 1.0)).astype(BF)
            return 0

        lax.fori_loop(0, 6, columns, 0)

        def outer(n, _):
            at = pl.ds(pl.multiple_of(n * 512, 512), 512)
            gctx[rows, at] = dg(cw[rows], wout[at, :], NT).astype(BF)
            return 0

        lax.fori_loop(0, 2, outer, 0)

    low_half = lax.broadcasted_iota(jnp.int32, (WINT, 128), 1) < 64
    zero = jnp.zeros((WINT, 128), BF)

    def unit(w, p, masked):
        rows = pl.ds(pl.multiple_of(w * WINT, 16), WINT)
        at_q = pl.ds(pl.multiple_of(p * 128, 128), 128)
        at_k = pl.ds(pl.multiple_of(1024 + p * 128, 128), 128)
        at_v = pl.ds(pl.multiple_of(2048 + p * 128, 128), 128)
        q, k, v, d = proj[rows, at_q], proj[rows, at_k], proj[rows, at_v], gctx[rows, at_q]
        ks = jnp.concatenate([jnp.where(low_half, k, zero), jnp.where(low_half, zero, k)], 0)
        vs = jnp.concatenate([jnp.where(low_half, v, zero), jnp.where(low_half, zero, v)], 0)
        offset = bias[pl.ds(2 * p, 2)]
        if masked is not None:
            offset = offset + mask[masked]
        st = dg(ks, q, NT).reshape(2, WINT, WINT) + offset
        powers = jnp.exp(st - jnp.max(st, axis=1, keepdims=True))
        weights = powers * (1.0 / jnp.sum(powers, axis=1, keepdims=True))
        wb = weights.astype(BF).reshape(PAIR, WINT)
        gctx[rows, at_q] = dg(wb, vs, TN).astype(BF)
        dw = dg(vs, d, NT).reshape(2, WINT, WINT)
        inner = jnp.sum(dw * weights, axis=1, keepdims=True)
        ds = (weights * (dw - inner)).astype(BF).reshape(PAIR, WINT)
        gv = dot(wb, d)
        gk = dot(ds, q)
        proj[rows, at_q] = (dg(ds, ks, TN) * 0.125).astype(BF)
        proj[rows, at_k] = jnp.where(low_half, gk[:WINT], gk[WINT:]).astype(BF)
        proj[rows, at_v] = jnp.where(low_half, gv[:WINT], gv[WINT:]).astype(BF)

    def late_windows(p):
        def two(t, _):
            masked = jnp.where(t == 0, 1, 0)
            unit(2 + 2 * t, p, masked)
            unit(3 + 2 * t, p, masked)
            return 0

        lax.fori_loop(0, 2, two, 0)

    def products(rnd, half, targets):
        def rows_of(zl, _):
            at = pl.multiple_of(zl * 512 + half * 256, 256)
            if rnd == 1:
                ct[...] = gctx[:, pl.ds(at, 256)].T
            for g in range(3):
                lane = 0
                for kind, first, width in PIECES[rnd][g]:
                    if kind == "in":
                        value = dot(nwt[pl.ds(at, 256), :], proj[:, first : first + width])
                    else:
                        value = dot(ct[...], cw[:, first : first + width])
                    value = value.reshape(32, 8, width)
                    wide = width // 2
                    both = jnp.concatenate([value[:, :, :wide], value[:, :, wide:]], 1)
                    targets[g][zl, :, :, :, :, lane : lane + wide] = both.astype(BF).reshape(2, 4, 4, 16, wide)
                    lane += wide
            return 0

        lax.fori_loop(0, 2, rows_of, 0)

    def start_core(rnd):
        return [
            remote(sends[rnd][g], halves[rnd][g], core_send.at[rnd, g], core_recv.at[rnd, g], sibling)
            for g in range(3)
        ]

    def end_core(rnd, copies):
        for g in range(3):
            copies[g].wait()
            owns[rnd][g][...] = (owns[rnd][g][...].astype(F32) + halves[rnd][g][...].astype(F32)).astype(BF)

    def source(rnd, g, phase):
        dims = ("zl", "zh", "x", "y")
        for axis in ORDERS[g][:phase]:
            dims = left_dims(dims, axis)
        return (owns[rnd][g] if phase == 0 else middles[rnd, g, phase - 1]), dims

    def chunk(rnd, g, phase, step, half):
        ref, dims = source(rnd, g, phase)
        axis = ORDERS[g][phase]
        t = (me[axis] + step + 4) % 4
        split = FIRST[rnd][g]
        end = (pl.ds(0, split), pl.ds(split, LANES[rnd][g] - split))[half]
        place = []
        for dim in dims:
            if dim == axis:
                place.append(t)
            elif axis == "z" and dim == "zl":
                place.append(t % 2)
            elif axis == "z" and dim == "zh":
                place.append(t // 2)
            else:
                place.append(slice(None))
        return ref.at[tuple(place) + (slice(None), end)]

    def ring(rnd, g, phase, number, src, step):
        return remote(
            src,
            landing[rnd, g, phase][number],
            ring_send.at[rnd, g, phase, number],
            ring_recv.at[rnd, g, phase, number],
            device(ORDERS[g][phase], step),
        )

    flying = {}

    def ring_start(rnd, phase):
        for g in range(3):
            flying[rnd, g] = {
                0: ring(rnd, g, phase, 0, chunk(rnd, g, phase, 2, 0), 1),
                3: ring(rnd, g, phase, 3, chunk(rnd, g, phase, 2, 1), -1),
                1: ring(rnd, g, phase, 1, chunk(rnd, g, phase, 1, 1), 1),
                4: ring(rnd, g, phase, 4, chunk(rnd, g, phase, -1, 0), -1),
            }

    def ring_relay(rnd, phase):
        for g in range(3):
            land = landing[rnd, g, phase]
            for number, step, half, slot in ((0, 1, 0, 6), (3, -1, 1, 7)):
                flying[rnd, g][number].wait_recv()
                land[slot][...] = (
                    land[number][...].astype(F32) + chunk(rnd, g, phase, step, half)[...].astype(F32)
                ).astype(BF)
                flying[rnd, g][number + 2] = ring(rnd, g, phase, number + 2, land[slot], step)

    def ring_end(rnd, phase):
        for g in range(3):
            land = landing[rnd, g, phase]
            copies = flying[rnd, g]
            for number in (1, 4, 2, 5):
                copies[number].wait()
            copies[0].wait_send()
            copies[3].wait_send()
            split = FIRST[rnd][g]
            for half, near, far in ((0, 4, 2), (1, 1, 5)):
                value = (
                    chunk(rnd, g, phase, 0, half)[...].astype(F32)
                    + land[near][...].astype(F32)
                    + land[far][...].astype(F32)
                ).astype(BF)
                start = half * split
                wide = value.shape[-1]
                if phase < 2:
                    middles[rnd, g, phase][..., start : start + wide] = value
                    continue
                lane = 0
                for kind, first, width in PIECES[rnd][g]:
                    low, high = max(start, lane), min(start + wide, lane + width // 2)
                    if low < high:
                        target = gi_out if kind == "in" else go_out
                        part = value[:, low - start : high - start]
                        at = first + low - lane
                        target[:, at : at + high - low] = part[:8]
                        at += width // 2
                        target[:, at : at + high - low] = part[8:]
                    lane += width // 2

    def gain_start(stage):
        if stage == 0:
            return [remote(gain_mine.at[0], gain_land.at[0], gain_send.at[0], gain_recv.at[0], sibling)]
        axis = AXES[stage - 1]
        slot = 3 * stage - 2
        return [
            remote(
                gain_mine.at[stage], gain_land.at[slot + n], gain_send.at[slot + n], gain_recv.at[slot + n], device(axis, s)
            )
            for n, s in ((0, 1), (1, -1))
        ]

    def gain_finish(stage, copies):
        total = gain_mine[stage]
        if stage == 0:
            copies[0].wait()
            return total + gain_land[0]
        slot = 3 * stage - 2
        copies[0].wait_recv()
        far = remote(
            gain_land.at[slot], gain_land.at[slot + 2], gain_send.at[slot + 2], gain_recv.at[slot + 2],
            device(AXES[stage - 1], 1),
        )
        copies[0].wait_send()
        copies[1].wait()
        far.wait()
        return total + gain_land[slot] + gain_land[slot + 1] + gain_land[slot + 2]

    def attended_step(s):
        rows = slice(s * PAIR, (s + 1) * PAIR)
        attended = dot(gctx[rows], wout[...]).astype(BF).astype(F32)
        xw_out[rows] = (xw[rows].astype(F32) + attended).astype(BF)

    def grad_step(s):
        rows = slice(s * PAIR, (s + 1) * PAIR)
        grad = dg(proj[rows], win[...], NT).astype(BF).astype(F32)
        standard, inverse = standardised(xw[rows].astype(F32))
        scaled = grad * gain_ref[...]
        first = jnp.mean(scaled, axis=-1, keepdims=True)
        second = jnp.mean(scaled * standard, axis=-1, keepdims=True)
        local = inverse * (scaled - first - standard * second)
        cw[rows] = (cw[rows].astype(F32) + local).astype(BF)
        return jnp.sum(grad * standard, axis=0, keepdims=True)

    def pack_back(number, final):
        both = dot(r1_ref[...], final[PAIR : 2 * PAIR]).astype(BF)
        send_strip[number][0:144] = both[:144]
        send_strip[number][288:384] = both[144:]
        send_strip[number][144:288] = dot(r2_ref[...], final[2 * PAIR :]).astype(BF)
        return send_strips(number, 1)

    def assemble(own, final, strip):
        value = dot(
            imid_ref[...], jnp.concatenate([final[:PAIR], final[2 * PAIR :], strip[144:288]], 0)
        ).astype(BF)
        own[72:360] = value[:288]
        own[504:792] = value[288:]
        value = dot(ibot_ref[...], jnp.concatenate([final[PAIR : 2 * PAIR], strip[288:336]], 0)).astype(BF)
        own[360:432] = value[:72]
        own[792:864] = value[72:]
        value = dot(itop_ref[...], jnp.concatenate([strip[0:144], strip[336:384]], 0)).astype(BF)
        own[0:72] = value[:72]
        own[432:504] = value[72:]

    xw_out = nw

    gather_step(0)
    for load in loads[2:]:
        load.wait()
    mask[0] = jnp.zeros((2, WINT, WINT), F32)
    mask[1] = jnp.where(lat == 3, 1.0, 0.0) * mask_ref[...].reshape(2, WINT, WINT)

    def turn(h, _):
        bias[h] = bias[h].T
        return 0

    lax.fori_loop(0, 16, turn, 0)
    project(0, PAIR)

    def early(p, _):
        unit(0, p, None)
        unit(1, p, None)
        return 0

    lax.fori_loop(0, 8, early, 0)
    for copies in strip_copies:
        for copy in copies:
            copy.wait()
    gather_step(1)
    gather_step(2)
    project(1, 2 * PAIR)

    def turn_rows(n, _):
        at = pl.ds(pl.multiple_of(n * 256, 256), 256)
        nwt[at, :] = nw[:, at].T
        return 0

    lax.fori_loop(0, 4, turn_rows, 0)

    def first_pairs(p, _):
        late_windows(p)
        return 0

    lax.fori_loop(0, 4, first_pairs, 0)
    products(0, 1 - core, sends[0])
    core_0 = start_core(0)
    products(0, core, owns[0])
    late_windows(4)
    end_core(0, core_0)
    ring_start(0, 0)
    late_windows(5)
    ring_relay(0, 0)
    late_windows(6)
    ring_end(0, 0)
    ring_start(0, 1)
    late_windows(7)
    ring_relay(0, 1)
    products(1, 1 - core, sends[1])
    core_1 = start_core(1)
    ring_end(0, 1)
    ring_start(0, 2)
    products(1, core, owns[1])
    ring_relay(0, 2)
    end_core(1, core_1)
    ring_start(1, 0)
    attended_step(1)
    attended_step(2)
    back_out = pack_back(2, xw_out)
    ring_end(0, 2)
    ring_relay(1, 0)
    gain = grad_step(1)
    gain += grad_step(2)
    back_grad = pack_back(3, cw)
    ring_end(1, 0)
    ring_start(1, 1)
    gain += grad_step(0)
    for n in range(8):
        gain_mine[0, n : n + 1, :] = gain[:, n * 128 : (n + 1) * 128]
    gain_copies = gain_start(0)
    ring_relay(1, 1)
    attended_step(0)
    gain_mine[1] = gain_finish(0, gain_copies)
    gain_copies = gain_start(1)
    ring_end(1, 1)
    ring_start(1, 2)
    for copy in back_out:
        copy.wait()
    assemble(own_x, xw_out, recv_strip[2])
    store_out = pltpu.make_async_copy(own_x, out_hbm, load_sem.at[0])
    store_out.start()
    gain_mine[2] = gain_finish(1, gain_copies)
    gain_copies = gain_start(2)
    ring_relay(1, 2)
    gain_mine[3] = gain_finish(2, gain_copies)
    gain_copies = gain_start(3)
    ring_end(1, 2)
    gg_out[...] = gain_finish(3, gain_copies)
    for copy in back_grad:
        copy.wait()
    assemble(own_c, cw, recv_strip[3])
    store_grad = pltpu.make_async_copy(own_c, gt_hbm, load_sem.at[1])
    store_grad.start()
    store_out.wait()
    store_grad.wait()


def block(tokens, cotangent, gain, attention_in, attention_out, head_bias):
    vm = pl.BlockSpec(memory_space=pltpu.VMEM)
    hbm = pl.BlockSpec(memory_space=pl.ANY)
    perms = [jnp.asarray(m, BF) for m in permutations()]
    wide = lambda rows, columns=D: pltpu.VMEM((rows, columns), BF)
    scratch = [wide(OWN) for _ in range(5)]
    scratch += [wide(D, OWN), wide(256, OWN), wide(OWN, 3 * D), wide(OWN), wide(D, 3 * D), wide(D)]
    scratch += [pltpu.VMEM((16, WINT, WINT), F32), pltpu.VMEM((2, 2, WINT, WINT), F32)]
    scratch += [wide(STRIP) for _ in range(8)]
    for _ in range(3):
        for r in range(2):
            scratch += [pltpu.VMEM((2, 2, 4, 4, 16, n), BF) for n in LANES[r]]
    middles = []
    for r in range(2):
        for g in range(3):
            dims = ("zl", "zh", "x", "y")
            a, b = FIRST[r][g], LANES[r][g] - FIRST[r][g]
            for phase in range(3):
                dims = left_dims(dims, ORDERS[g][phase])
                lead = tuple(SIZES[d] for d in dims)
                scratch += [pltpu.VMEM(lead + (16, n), BF) for n in (a, b, a, b, a, b, a, b)]
                if phase < 2:
                    middles.append(pltpu.VMEM(lead + (16, a + b), BF))
    scratch += middles
    scratch += [pltpu.VMEM((4, 8, 128), F32), pltpu.VMEM((10, 8, 128), F32)]
    dma = pltpu.SemaphoreType.DMA
    scratch += [dma((5,)), dma((4, 3)), dma((4, 3)), dma((2, 3)), dma((2, 3))]
    scratch += [dma((2, 3, 3, 6)), dma((2, 3, 3, 6)), dma((10,)), dma((10,))]
    return pl.pallas_call(
        block_kernel,
        in_specs=[hbm, hbm, vm, hbm, hbm, hbm, vm] + [vm] * 9,
        out_specs=[hbm, hbm, vm, vm, vm],
        out_shape=[
            jax.ShapeDtypeStruct((OWN, D), BF),
            jax.ShapeDtypeStruct((OWN, D), BF),
            jax.ShapeDtypeStruct((8, 3 * D), BF),
            jax.ShapeDtypeStruct((8, D), BF),
            jax.ShapeDtypeStruct((8, 128), F32),
        ],
        scratch_shapes=scratch,
        compiler_params=pltpu.CompilerParams(
            collective_id=0, has_side_effects=True, vmem_limit_bytes=63 * 2**20
        ),
    )(
        tokens, cotangent, gain.reshape(1, D), attention_in, attention_out, head_bias,
        jnp.asarray(region_mask()), *perms,
    )


def local(tokens, norm_gain, attention_in, attention_out, head_bias, cotangent):
    shape = tokens.shape
    lat = lax.axis_index("lat")
    lon = lax.axis_index("lon")
    out, gt, gi, go, gains = block(
        tokens.reshape(OWN, D), cotangent.reshape(OWN, D), norm_gain, attention_in, attention_out, head_bias
    )
    gain = lax.dynamic_slice(gains.reshape(1024), ((lat * 32 + lon) * 8,), (8,))
    return out.reshape(shape), gt.reshape(shape), gi, go, gain


def solution(mesh):
    split = P(None, "lat", "lon", None)
    both = ("lat", "lon")
    return jax.shard_map(
        local,
        mesh=mesh,
        in_specs=(split, P(), P(), P(), P(), split),
        out_specs=(split, split, P(both, None), P(both, None), P(both)),
        check_vma=False,
    )
```

time: 1800 us -> 152 us (0.08)
  the two profiles are of different devices: /device:TPU:96 before, /device:TPU:48 now
where the time goes in v1:
time: 152 us
  Pallas kernels  145 us (95%)
  local copies, waits for them, and re-layouts  6.67 us (4%)
    pallas_call x1, Pallas kernels, block(): pl.pallas_call(block_kernel, in_specs=[hbm, hbm, vm, hbm, hbm, hbm, vm] +...  145 us
    unnamed x10, local copies, waits for them, and re-layouts  5.41 us

profile of v1, /device:TPU:48, one launch (start us, length us, event | category | flops | bytes accessed | tf_op | source)
XLA Modules:
  0.0 151.9 jit_solution(625717354828972055)
XLA Ops:
  0.6 144.6 %shard_map.191 = (bf16[864,1024]{1,0:T(8,128)(2,1)}, bf16[864,1024]{1,0:T(8,128)(2,1)}, bf16[8,3072]{1,0:T(8,128)(2,1)}, bf16[8,1024]{1,0:T(8,128)(2,1)}, f32[8,128]{1,0:T(8,128)}) custom-call(bf16[864,1024]{1,0:T(8,128)(2,1)} %bitcast.6, bf16[864,1024]{1,0:T(8,128)(2,1)} %bitcast.7, f32[1,1024]{1,0:T(1,128)} %bitcast.10, bf16[1024,3072]{1,0:T(8,128)(2,1)} %win_hbm.1, ...), custom_call_target="tpu_custom_call" | custom-call | tf_op jit(solution)/shard_map/pallas_call | solution.py:605
  145.2 1.3 dynamic_slice.3
  146.5 0.0 copy-start
  146.5 3.0 %copy.25 = bf16[2,18,24,1024]{3,2,1,0:T(8,128)(2,1)} copy(bf16[2,18,24,1024]{3,2,1,0:T(8,128)(2,1)} %bitcast.9) | data formatting | bytes 3538944
  149.4 0.0 copy-done
  149.5 0.0 copy-start.1
  149.5 0.0 copy-start.2
  149.5 1.2 copy.26
  150.7 0.0 copy-done.1
  150.7 0.6 copy.27
  151.3 0.0 copy-done.2
  151.3 0.6 copy.28
Async XLA Ops:
  146.5 3.0 %copy-start = (bf16[864,1024]{1,0:T(8,128)(2,1)S(1)}, bf16[864,1024]{1,0:T(8,128)(2,1)}, u32[]{:S(2)}) copy-start(bf16[864,1024]{1,0:T(8,128)(2,1)} %get-tuple-element.11) | copy-start | bytes 5308420
  149.5 1.2 copy-start.1
  149.5 1.8 %copy-start.2 = (bf16[8,1024]{1,0:T(8,128)(2,1)S(1)}, bf16[8,1024]{1,0:T(8,128)(2,1)}, u32[]{:S(2)}) copy-start(bf16[8,1024]{1,0:T(8,128)(2,1)} %get-tuple-element.23) | copy-start | bytes 49156

commit v2 on v1

v2 whole, which is shorter than its diff:
```python
import jax
import jax.numpy as jnp
import numpy as np
from jax import lax
from jax.experimental import pallas as pl
from jax.experimental.pallas import tpu as pltpu
from jax.sharding import PartitionSpec as P

D = 1024
WINT = 144
PAIR = 288
OWN = 864
STRIP = 400
NT = (((1,), (1,)), ((), ()))
TN = (((0,), (0,)), ((), ()))
BF = jnp.bfloat16
F32 = jnp.float32

AXES = ("x", "y", "z")
ORDERS = (
    (("x", "y", "z"), ("y", "z", "x"), ("z", "x", "y")),
    (("x", "y", "z"), ("y", "z", "x"), ("z", "x", "y")),
    (("x", "z", "y"), ("z", "x", "y")),
)
PIECES = (
    tuple(("in", 1024 * g, 512) for g in range(3)),
    tuple(("in", 1024 * g + 512, 512) for g in range(3)),
    tuple(("out", 512 * g, 512) for g in range(2)),
)
LANES = 256
FIRST = 128
GROUPS = tuple((r, g) for r in range(3) for g in range(len(ORDERS[r])))
SIZES = {"zl": 2, "zh": 2, "x": 4, "y": 4}


def left_dims(dims, axis):
    gone = ("zl", "zh") if axis == "z" else (axis,)
    return tuple(d for d in dims if d not in gone)


def strip_cells(core):
    cells = [(l, r, c) for l in range(2) for r in range(3) for c in range(24)]
    cells += [(l, r, c) for l in range(2) for r in range(3, 9) for c in range(18, 24)] + [None] * 8
    first = 0 if core else 18
    cells += [(l, r, c) for l in range(2) for r in range(9, 15) for c in range(first, first + 6)] + [None] * 8
    cells += [(l, r, c) for l in range(2) for r in range(15, 18) for c in range(6)] + [None] * 12
    cells += [(l, r, c) for l in range(2) for r in range(3) for c in range(6)] + [None] * 12
    return cells


def received_cells(core):
    cells = []
    for n, cell in enumerate(strip_cells(core)):
        if cell is None:
            cells.append(None)
            continue
        l, r, c = cell
        if n < 144 or n >= 352:
            r += 18
        if n >= 144:
            c += 24 if c < 6 else -24
        cells.append((l, r, c))
    return cells


def window_cells(core):
    corners = ((3, 6), (9, 6), (15, 6), (15, 18), (3, -6), (9, 18 if core else -6))
    return [(l, r + a, c + b) for r, c in corners for l in range(2) for a in range(6) for b in range(12)]


def one_hot(targets, sources):
    place = {}
    for n, cell in enumerate(sources):
        if cell is not None and cell not in place:
            place[cell] = n
    out = np.zeros((len(targets), len(sources)), np.float32)
    for n, cell in enumerate(targets):
        if cell is not None and cell in place:
            out[n, place[cell]] = 1
    return out


def permutations():
    own = [(l, r, c) for l in range(2) for r in range(18) for c in range(24)]
    wide = own[64:368] + own[496:800]
    mid = own[72:360] + own[504:792]
    bottom = own[360:432] + own[792:864]
    top = own[:72] + own[432:504]
    every = []
    for core in range(2):
        strips = strip_cells(core)
        got = received_cells(core)
        win = window_cells(core)
        inner = [c if c is not None and c[2] >= 6 else None for c in strips[:144]]
        every.append(
            (
                one_hot(strips, own),
                one_hot(win[:288], wide),
                one_hot(win[288:576], own[352:432] + own[784:864] + got[:144] + got[304:]),
                one_hot(win[576:], wide + got[144:304]),
                one_hot(got[:144] + got[304:], win[288:576]),
                one_hot(got[144:304], win[576:]),
                one_hot(mid, win[:288] + win[576:] + strips[144:304]),
                one_hot(bottom, win[288:576] + strips[304:352]),
                one_hot(top, inner + strips[352:]),
            )
        )
    return tuple(np.stack(pair) for pair in zip(*every))


def region_mask():
    region = np.array([a < 3 for l in range(2) for a in range(6) for b in range(12)])
    one = np.where(region[:, None] == region[None, :], 0.0, -1e9).astype(np.float32)
    return np.concatenate([one, one], 0)


def dg(a, b, dims):
    return lax.dot_general(a, b, dims, preferred_element_type=F32)


def dot(a, b):
    return jnp.dot(a, b, preferred_element_type=F32)


def mesh_place(core, x, y, z):
    return ((z % 2) * 2 + core, (z // 2) * 16 + x * 4 + y)


def block_kernel(
    tok_hbm, cot_hbm, gain_ref, win_hbm, wout_hbm, hb_hbm, mask_ref,
    pack_hbm, p0_hbm, p1_hbm, p2_hbm, r1_hbm, r2_hbm, imid_hbm, ibot_hbm, itop_hbm,
    out_hbm, gt_hbm, gi_out, go_out, gg_out,
    *scratch,
):
    scratch = list(scratch)

    def take(count):
        out = scratch[:count]
        del scratch[:count]
        return out

    own_x, own_c, xw, cw, nw, nwt, proj, gctx, win, wout, bias, mask = take(12)
    perms = take(9)
    pack_ref, p0_ref, p1_ref, p2_ref, r1_ref, r2_ref, imid_ref, ibot_ref, itop_ref = perms
    send_strip, recv_strip = take(4), take(4)
    sends = {at: take(1)[0] for at in GROUPS}
    owns = {at: take(1)[0] for at in GROUPS}
    halves = {at: take(1)[0] for at in GROUPS}
    landing = {(r, g, p): take(8) for r, g in GROUPS for p in range(3)}
    middles = {(r, g, p): take(1)[0] for r, g in GROUPS for p in range(2)}
    gain_mine, gain_land = take(2)
    load_sem, strip_send, strip_recv, core_send, core_recv = take(5)
    ring_send, ring_recv, gain_send, gain_recv = take(4)

    lat = lax.axis_index("lat")
    lon = lax.axis_index("lon")
    core = lat % 2
    me = {"x": (lon // 4) % 4, "y": lon % 4, "z": (lon // 16) * 2 + lat // 2}

    def device(axis, step):
        at = dict(me)
        at[axis] = (me[axis] + step + 4) % 4
        return mesh_place(core, at["x"], at["y"], at["z"])

    sibling = mesh_place(1 - core, me["x"], me["y"], me["z"])

    def grid_place(a, b):
        return ((lat + a + 4) % 4, (lon + b + 32) % 32)

    loads = [
        pltpu.make_async_copy(src, dst, load_sem.at[n])
        for n, (src, dst) in enumerate(
            (
                (tok_hbm, own_x), (pack_hbm.at[core], pack_ref), (cot_hbm, own_c), (p0_hbm.at[core], p0_ref),
                (win_hbm, win), (wout_hbm, wout), (hb_hbm, bias), (p1_hbm.at[core], p1_ref), (p2_hbm.at[core], p2_ref),
                (r1_hbm.at[core], r1_ref), (r2_hbm.at[core], r2_ref), (imid_hbm.at[core], imid_ref),
                (ibot_hbm.at[core], ibot_ref), (itop_hbm.at[core], itop_ref),
            )
        )
    ]
    for load in loads:
        load.start()

    barrier = pltpu.get_barrier_semaphore()
    partners = [sibling] + [device(a, s) for a in AXES for s in (1, -1, 2)]
    partners += [grid_place(s * a, s * b) for a, b in ((1, 0), (0, 1), (1, 1)) for s in (1, -1)]
    for other in partners:
        pl.semaphore_signal(barrier, inc=1, device_id=other, device_id_type=pl.DeviceIdType.MESH)
    pl.semaphore_wait(barrier, len(partners))

    def remote(src, dst, send, recv, place):
        copy = pltpu.make_async_remote_copy(
            src_ref=src,
            dst_ref=dst,
            send_sem=send,
            recv_sem=recv,
            device_id=place,
            device_id_type=pl.DeviceIdType.MESH,
        )
        copy.start()
        return copy

    turned = jnp.where(core == 0, 1, -1)
    PARTS = ((0, 144, -1, 0), (144, 80, 0, 1), (224, 80, 0, turned), (304, 48, 0, -1), (352, 48, -1, -1))

    def send_strips(number, way, parts=range(5)):
        copies = []
        for part in parts:
            low, size, a, b = PARTS[part]
            copies.append(
                remote(
                    send_strip[number].at[pl.ds(low, size)],
                    recv_strip[number].at[pl.ds(low, size)],
                    strip_send.at[number, part],
                    strip_recv.at[number, part],
                    grid_place(way * a, way * b),
                )
            )
        return copies

    strip_copies = []
    loads[0].wait()
    loads[1].wait()
    for number, own in ((0, own_x), (1, own_c)):
        if number == 1:
            loads[2].wait()
        send_strip[number][...] = dot(pack_ref[...], own[...]).astype(BF)
        strip_copies.append(send_strips(number, 1))

    def gathered(own, strip, s):
        if s == 1:
            parts = [own[352:432], own[784:864], strip[0:144], strip[304:400]]
            return dot(p1_ref[...], jnp.concatenate(parts, 0))
        parts = [own[64:368], own[496:800]]
        if s == 0:
            return dot(p0_ref[...], jnp.concatenate(parts, 0))
        return dot(p2_ref[...], jnp.concatenate(parts + [strip[144:304]], 0))

    def standardised(x):
        centred = x - jnp.mean(x, axis=-1, keepdims=True)
        inverse = lax.rsqrt(jnp.mean(centred * centred, axis=-1, keepdims=True) + 1e-5)
        return centred * inverse, inverse

    def gather_tokens(s):
        rows = slice(s * PAIR, (s + 1) * PAIR)
        x = gathered(own_x, recv_strip[0], s)
        xw[rows] = x.astype(BF)
        standard, _ = standardised(x)
        nw[rows] = (standard * gain_ref[...]).astype(BF)

    def gather_cotangent(s):
        rows = slice(s * PAIR, (s + 1) * PAIR)
        cw[rows] = gathered(own_c, recv_strip[1], s).astype(BF)

    def project(s, count):
        rows = slice(s * PAIR, s * PAIR + count)

        def columns(n, _):
            at = pl.ds(pl.multiple_of(n * 512, 512), 512)
            value = dot(nw[rows], win[:, at])
            proj[rows, at] = (value * jnp.where(n < 2, 0.125, 1.0)).astype(BF)
            return 0

        lax.fori_loop(0, 6, columns, 0)

    def project_back(s, count):
        rows = slice(s * PAIR, s * PAIR + count)

        def outer(n, _):
            at = pl.ds(pl.multiple_of(n * 512, 512), 512)
            gctx[rows, at] = dg(cw[rows], wout[at, :], NT).astype(BF)
            return 0

        lax.fori_loop(0, 2, outer, 0)

    low_half = lax.broadcasted_iota(jnp.int32, (WINT, 128), 1) < 64
    zero = jnp.zeros((WINT, 128), BF)

    def unit(w, p, masked):
        rows = pl.ds(pl.multiple_of(w * WINT, 16), WINT)
        at_q = pl.ds(pl.multiple_of(p * 128, 128), 128)
        at_k = pl.ds(pl.multiple_of(1024 + p * 128, 128), 128)
        at_v = pl.ds(pl.multiple_of(2048 + p * 128, 128), 128)
        q, k, v, d = proj[rows, at_q], proj[rows, at_k], proj[rows, at_v], gctx[rows, at_q]
        ks = jnp.concatenate([jnp.where(low_half, k, zero), jnp.where(low_half, zero, k)], 0)
        vs = jnp.concatenate([jnp.where(low_half, v, zero), jnp.where(low_half, zero, v)], 0)
        offset = bias[pl.ds(2 * p, 2)]
        if masked is not None:
            offset = offset + mask[masked]
        st = dg(ks, q, NT).reshape(2, WINT, WINT) + offset
        powers = jnp.exp(st - jnp.max(st, axis=1, keepdims=True))
        weights = powers * (1.0 / jnp.sum(powers, axis=1, keepdims=True))
        wb = weights.astype(BF).reshape(PAIR, WINT)
        gctx[rows, at_q] = dg(wb, vs, TN).astype(BF)
        dw = dg(vs, d, NT).reshape(2, WINT, WINT)
        inner = jnp.sum(dw * weights, axis=1, keepdims=True)
        ds = (weights * (dw - inner)).astype(BF).reshape(PAIR, WINT)
        gv = dot(wb, d)
        gk = dot(ds, q)
        proj[rows, at_q] = (dg(ds, ks, TN) * 0.125).astype(BF)
        proj[rows, at_k] = jnp.where(low_half, gk[:WINT], gk[WINT:]).astype(BF)
        proj[rows, at_v] = jnp.where(low_half, gv[:WINT], gv[WINT:]).astype(BF)

    def late_windows(p):
        def two(t, _):
            masked = jnp.where(t == 0, 1, 0)
            unit(2 + 2 * t, p, masked)
            unit(3 + 2 * t, p, masked)
            return 0

        lax.fori_loop(0, 2, two, 0)

    def products(rnd, g, half, target):
        kind, first, width = PIECES[rnd][g]
        right = proj if kind == "in" else cw

        def rows_of(zl, _):
            at = pl.multiple_of(zl * 512 + half * 256, 256)
            value = dot(nwt[pl.ds(at, 256), :], right[:, first : first + width]).reshape(32, 8, width)
            both = jnp.concatenate([value[:, :, :LANES], value[:, :, LANES:]], 1)
            target[zl] = both.astype(BF).reshape(2, 4, 4, 16, LANES)
            return 0

        lax.fori_loop(0, 2, rows_of, 0)

    core_copies = {}

    def start_round(rnd):
        for g in range(len(ORDERS[rnd])):
            products(rnd, g, 1 - core, sends[rnd, g])
            core_copies[rnd, g] = remote(
                sends[rnd, g], halves[rnd, g], core_send.at[rnd, g], core_recv.at[rnd, g], sibling
            )

    def own_products(rnd):
        for g in range(len(ORDERS[rnd])):
            products(rnd, g, core, owns[rnd, g])

    def end_core(rnd):
        for g in range(len(ORDERS[rnd])):
            core_copies[rnd, g].wait()
            mine = owns[rnd, g]
            mine[...] = (mine[...].astype(F32) + halves[rnd, g][...].astype(F32)).astype(BF)
            ring_start_group(rnd, g, 0)

    def source(rnd, g, phase):
        dims = ("zl", "zh", "x", "y")
        for axis in ORDERS[rnd][g][:phase]:
            dims = left_dims(dims, axis)
        return (owns[rnd, g] if phase == 0 else middles[rnd, g, phase - 1]), dims

    def chunk(rnd, g, phase, step, half):
        ref, dims = source(rnd, g, phase)
        axis = ORDERS[rnd][g][phase]
        t = (me[axis] + step + 4) % 4
        end = pl.ds(half * FIRST, FIRST)
        place = []
        for dim in dims:
            if dim == axis:
                place.append(t)
            elif axis == "z" and dim == "zl":
                place.append(t % 2)
            elif axis == "z" and dim == "zh":
                place.append(t // 2)
            else:
                place.append(slice(None))
        return ref.at[tuple(place) + (slice(None), end)]

    def ring(rnd, g, phase, number, src, step):
        return remote(
            src,
            landing[rnd, g, phase][number],
            ring_send.at[rnd, g, phase, number],
            ring_recv.at[rnd, g, phase, number],
            device(ORDERS[rnd][g][phase], step),
        )

    flying = {}

    def ring_start_group(rnd, g, phase):
        flying[rnd, g] = {
            0: ring(rnd, g, phase, 0, chunk(rnd, g, phase, 2, 0), 1),
            3: ring(rnd, g, phase, 3, chunk(rnd, g, phase, 2, 1), -1),
            1: ring(rnd, g, phase, 1, chunk(rnd, g, phase, 1, 1), 1),
            4: ring(rnd, g, phase, 4, chunk(rnd, g, phase, -1, 0), -1),
        }

    def ring_relay(rnd, phase):
        for g in range(len(ORDERS[rnd])):
            land = landing[rnd, g, phase]
            for number, step, half, slot in ((0, 1, 0, 6), (3, -1, 1, 7)):
                flying[rnd, g][number].wait_recv()
                land[slot][...] = (
                    land[number][...].astype(F32) + chunk(rnd, g, phase, step, half)[...].astype(F32)
                ).astype(BF)
                flying[rnd, g][number + 2] = ring(rnd, g, phase, number + 2, land[slot], step)

    def ring_end(rnd, phase):
        for g in range(len(ORDERS[rnd])):
            land = landing[rnd, g, phase]
            copies = flying[rnd, g]
            for number in (1, 4, 2, 5):
                copies[number].wait()
            copies[0].wait_send()
            copies[3].wait_send()
            for half, near, far in ((0, 4, 2), (1, 1, 5)):
                value = (
                    chunk(rnd, g, phase, 0, half)[...].astype(F32)
                    + land[near][...].astype(F32)
                    + land[far][...].astype(F32)
                ).astype(BF)
                start = half * FIRST
                if phase < 2:
                    middles[rnd, g, phase][..., start : start + FIRST] = value
                    continue
                kind, first, _ = PIECES[rnd][g]
                target = gi_out if kind == "in" else go_out
                target[:, first + start : first + start + FIRST] = value[:8]
                target[:, first + LANES + start : first + LANES + start + FIRST] = value[8:]
            if phase < 2:
                ring_start_group(rnd, g, phase + 1)

    def gain_start(stage):
        if stage == 0:
            return [remote(gain_mine.at[0], gain_land.at[0], gain_send.at[0], gain_recv.at[0], sibling)]
        return [
            remote(
                gain_mine.at[stage],
                gain_land.at[3 * stage - 2 + n],
                gain_send.at[3 * stage - 2 + n],
                gain_recv.at[3 * stage - 2 + n],
                device(AXES[stage - 1], n + 1),
            )
            for n in range(3)
        ]

    def gain_finish(stage, copies):
        total = gain_mine[stage]
        for copy in copies:
            copy.wait()
        if stage == 0:
            return total + gain_land[0]
        slot = 3 * stage - 2
        return total + gain_land[slot] + gain_land[slot + 1] + gain_land[slot + 2]

    def attended_step(s):
        rows = slice(s * PAIR, (s + 1) * PAIR)
        attended = dot(gctx[rows], wout[...]).astype(BF).astype(F32)
        xw_out[rows] = (xw[rows].astype(F32) + attended).astype(BF)

    def grad_step(s):
        rows = slice(s * PAIR, (s + 1) * PAIR)
        grad = dg(proj[rows], win[...], NT).astype(BF).astype(F32)
        standard, inverse = standardised(xw[rows].astype(F32))
        scaled = grad * gain_ref[...]
        first = jnp.mean(scaled, axis=-1, keepdims=True)
        second = jnp.mean(scaled * standard, axis=-1, keepdims=True)
        local = inverse * (scaled - first - standard * second)
        cw[rows] = (cw[rows].astype(F32) + local).astype(BF)
        return jnp.sum(grad * standard, axis=0, keepdims=True)

    def pack_back(number, final):
        both = dot(r1_ref[...], final[PAIR : 2 * PAIR]).astype(BF)
        send_strip[number][0:144] = both[:144]
        send_strip[number][304:400] = both[144:]
        send_strip[number][144:304] = dot(r2_ref[...], final[2 * PAIR :]).astype(BF)
        return send_strips(number, -1)

    def assemble(own, final, strip):
        value = dot(
            imid_ref[...], jnp.concatenate([final[:PAIR], final[2 * PAIR :], strip[144:304]], 0)
        ).astype(BF)
        own[72:360] = value[:288]
        own[504:792] = value[288:]
        value = dot(ibot_ref[...], jnp.concatenate([final[PAIR : 2 * PAIR], strip[304:352]], 0)).astype(BF)
        own[360:432] = value[:72]
        own[792:864] = value[72:]
        value = dot(itop_ref[...], jnp.concatenate([strip[0:144], strip[352:400]], 0)).astype(BF)
        own[0:72] = value[:72]
        own[432:504] = value[72:]

    xw_out = nw

    loads[3].wait()
    gather_tokens(0)
    gather_cotangent(0)
    for load in loads[4:]:
        load.wait()
    mask[0] = jnp.zeros((2, WINT, WINT), F32)
    mask[1] = jnp.where(lat == 3, 1.0, 0.0) * mask_ref[...].reshape(2, WINT, WINT)

    def turn(h, _):
        bias[h] = bias[h].T
        return 0

    lax.fori_loop(0, 16, turn, 0)
    project(0, PAIR)
    project_back(0, PAIR)

    def early(p, _):
        unit(0, p, None)
        unit(1, p, None)
        return 0

    lax.fori_loop(0, 8, early, 0)
    for copy in strip_copies[0]:
        copy.wait()
    gather_tokens(1)
    gather_tokens(2)
    project(1, 2 * PAIR)

    def turn_rows(n, _):
        at = pl.ds(pl.multiple_of(n * 256, 256), 256)
        nwt[at, :] = nw[:, at].T
        return 0

    lax.fori_loop(0, 4, turn_rows, 0)
    for copy in strip_copies[1]:
        copy.wait()
    gather_cotangent(1)
    gather_cotangent(2)
    project_back(1, 2 * PAIR)

    def first_pairs(p, _):
        late_windows(p)
        return 0

    lax.fori_loop(0, 4, first_pairs, 0)
    start_round(0)
    own_products(0)
    late_windows(4)
    end_core(0)
    late_windows(5)
    ring_relay(0, 0)
    late_windows(6)
    ring_end(0, 0)
    late_windows(7)
    ring_relay(0, 1)
    start_round(1)
    ring_end(0, 1)
    own_products(1)
    ring_relay(0, 2)
    attended_step(1)
    attended_step(2)
    back_out = pack_back(2, xw_out)
    end_core(1)

    def turn_context(n, _):
        at = pl.ds(pl.multiple_of(n * 256, 256), 256)
        nwt[at, :] = gctx[:, at].T
        return 0

    lax.fori_loop(0, 4, turn_context, 0)
    start_round(2)
    own_products(2)
    gain = grad_step(1)
    ring_relay(1, 0)
    gain += grad_step(2)
    back_grad = pack_back(3, cw)
    end_core(2)
    gain += grad_step(0)
    for n in range(8):
        gain_mine[0, n : n + 1, :] = gain[:, n * 128 : (n + 1) * 128]
    gain_copies = gain_start(0)
    ring_end(1, 0)
    ring_relay(2, 0)
    attended_step(0)
    ring_end(0, 2)
    gain_mine[1] = gain_finish(0, gain_copies)
    gain_copies = gain_start(1)
    ring_relay(1, 1)
    ring_end(2, 0)
    for copy in back_out:
        copy.wait()
    assemble(own_x, xw_out, recv_strip[2])
    store_out = pltpu.make_async_copy(own_x, out_hbm, load_sem.at[0])
    store_out.start()
    gain_mine[2] = gain_finish(1, gain_copies)
    gain_copies = gain_start(2)
    ring_end(1, 1)
    ring_relay(2, 1)
    gain_mine[3] = gain_finish(2, gain_copies)
    gain_copies = gain_start(3)
    ring_relay(1, 2)
    ring_end(2, 1)
    for copy in back_grad:
        copy.wait()
    assemble(own_c, cw, recv_strip[3])
    store_grad = pltpu.make_async_copy(own_c, gt_hbm, load_sem.at[1])
    store_grad.start()
    ring_relay(2, 2)
    gg_out[...] = gain_finish(3, gain_copies)
    ring_end(1, 2)
    ring_end(2, 2)
    store_out.wait()
    store_grad.wait()


def block(tokens, cotangent, gain, attention_in, attention_out, head_bias):
    vm = pl.BlockSpec(memory_space=pltpu.VMEM)
    hbm = pl.BlockSpec(memory_space=pl.ANY)
    perms = [jnp.asarray(m, BF) for m in permutations()]
    wide = lambda rows, columns=D: pltpu.VMEM((rows, columns), BF)
    scratch = [wide(OWN) for _ in range(5)]
    scratch += [wide(D, OWN), wide(OWN, 3 * D), wide(OWN), wide(D, 3 * D), wide(D)]
    scratch += [pltpu.VMEM((16, WINT, WINT), F32), pltpu.VMEM((2, 2, WINT, WINT), F32)]
    scratch += [wide(*m.shape[1:]) for m in perms]
    scratch += [wide(STRIP) for _ in range(8)]
    scratch += [pltpu.VMEM((2, 2, 4, 4, 16, LANES), BF) for _ in range(3 * len(GROUPS))]
    middles = []
    for r, g in GROUPS:
        dims = ("zl", "zh", "x", "y")
        for phase in range(3):
            dims = left_dims(dims, ORDERS[r][g][phase])
            lead = tuple(SIZES[d] for d in dims)
            scratch += [pltpu.VMEM(lead + (16, FIRST), BF) for _ in range(8)]
            if phase < 2:
                middles.append(pltpu.VMEM(lead + (16, LANES), BF))
    scratch += middles
    scratch += [pltpu.VMEM((4, 8, 128), F32), pltpu.VMEM((10, 8, 128), F32)]
    dma = pltpu.SemaphoreType.DMA
    scratch += [dma((14,)), dma((4, 5)), dma((4, 5)), dma((3, 3)), dma((3, 3))]
    scratch += [dma((3, 3, 3, 6)), dma((3, 3, 3, 6)), dma((10,)), dma((10,))]
    return pl.pallas_call(
        block_kernel,
        in_specs=[hbm, hbm, vm, hbm, hbm, hbm, vm] + [hbm] * 9,
        out_specs=[hbm, hbm, vm, vm, vm],
        out_shape=[
            jax.ShapeDtypeStruct((OWN, D), BF),
            jax.ShapeDtypeStruct((OWN, D), BF),
            jax.ShapeDtypeStruct((8, 3 * D), BF),
            jax.ShapeDtypeStruct((8, D), BF),
            jax.ShapeDtypeStruct((8, 128), F32),
        ],
        scratch_shapes=scratch,
        compiler_params=pltpu.CompilerParams(
            collective_id=0, has_side_effects=True, vmem_limit_bytes=63 * 2**20
        ),
    )(
        tokens, cotangent, gain.reshape(1, D), attention_in, attention_out, head_bias,
        jnp.asarray(region_mask()), *perms,
    )


def local(tokens, norm_gain, attention_in, attention_out, head_bias, cotangent):
    shape = tokens.shape
    lat = lax.axis_index("lat")
    lon = lax.axis_index("lon")
    out, gt, gi, go, gains = block(
        tokens.reshape(OWN, D), cotangent.reshape(OWN, D), norm_gain, attention_in, attention_out, head_bias
    )
    gain = lax.dynamic_slice(gains.reshape(1024), ((lat * 32 + lon) * 8,), (8,))
    return out.reshape(shape), gt.reshape(shape), gi, go, gain


def solution(mesh):
    split = P(None, "lat", "lon", None)
    both = ("lat", "lon")
    return jax.shard_map(
        local,
        mesh=mesh,
        in_specs=(split, P(), P(), P(), P(), split),
        out_specs=(split, split, P(both, None), P(both, None), P(both)),
        check_vma=False,
    )
```

time: 152 us -> 135 us (0.89)
  the two profiles are of different devices: /device:TPU:48 before, /device:TPU:1 now
where the time goes in v2:
time: 135 us
  Pallas kernels  127 us (94%)
  local copies, waits for them, and re-layouts  6.67 us (5%)
    pallas_call x1, Pallas kernels, block(): pl.pallas_call(block_kernel, in_specs=[hbm, hbm, vm, hbm, hbm, hbm, vm] +...  127 us
    unnamed x10, local copies, waits for them, and re-layouts  5.41 us

profile of v2, /device:TPU:1, one launch (start us, length us, event | category | flops | bytes accessed | tf_op | source)
XLA Modules:
  0.0 134.7 jit_solution(5604598138046335303)
XLA Ops:
  0.6 127.4 %shard_map.191 = (bf16[864,1024]{1,0:T(8,128)(2,1)}, bf16[864,1024]{1,0:T(8,128)(2,1)}, bf16[8,3072]{1,0:T(8,128)(2,1)}, bf16[8,1024]{1,0:T(8,128)(2,1)}, f32[8,128]{1,0:T(8,128)}) custom-call(bf16[864,1024]{1,0:T(8,128)(2,1)} %bitcast.8, bf16[864,1024]{1,0:T(8,128)(2,1)} %bitcast.9, f32[1,1024]{1,0:T(1,128)} %bitcast.10, bf16[1024,3072]{1,0:T(8,128)(2,1)} %win_hbm.1, ...), custom_call_target="tpu_custom_call" | custom-call | tf_op jit(solution)/shard_map/pallas_call | solution.py:624
  128.1 1.3 dynamic_slice.3
  129.3 0.0 copy-start
  129.3 3.0 %copy.25 = bf16[2,18,24,1024]{3,2,1,0:T(8,128)(2,1)} copy(bf16[2,18,24,1024]{3,2,1,0:T(8,128)(2,1)} %bitcast.7) | data formatting | bytes 3538944
  132.3 0.0 copy-done
  132.3 0.0 copy-start.1
  132.3 0.0 copy-start.2
  132.3 1.2 copy.26
  133.5 0.0 copy-done.1
  133.5 0.6 copy.27
  134.1 0.0 copy-done.2
  134.1 0.6 copy.28
Async XLA Ops:
  129.3 3.0 %copy-start = (bf16[864,1024]{1,0:T(8,128)(2,1)S(1)}, bf16[864,1024]{1,0:T(8,128)(2,1)}, u32[]{:S(2)}) copy-start(bf16[864,1024]{1,0:T(8,128)(2,1)} %get-tuple-element.11) | copy-start | bytes 5308420
  132.3 1.2 copy-start.1
  132.3 1.8 %copy-start.2 = (bf16[8,1024]{1,0:T(8,128)(2,1)S(1)}, bf16[8,1024]{1,0:T(8,128)(2,1)}, u32[]{:S(2)}) copy-start(bf16[8,1024]{1,0:T(8,128)(2,1)} %get-tuple-element.23) | copy-start | bytes 49156

commit v3 on v2

--- a/solution.py
+++ b/solution.py
@@ -30,12 +30,6 @@
 LANES = 256
 FIRST = 128
 GROUPS = tuple((r, g) for r in range(3) for g in range(len(ORDERS[r])))
-SIZES = {"zl": 2, "zh": 2, "x": 4, "y": 4}
-
-
-def left_dims(dims, axis):
-    gone = ("zl", "zh") if axis == "z" else (axis,)
-    return tuple(d for d in dims if d not in gone)
 
 
 def strip_cells(core):
@@ -139,7 +133,7 @@
         del scratch[:count]
         return out
 
-    own_x, own_c, xw, cw, nw, nwt, proj, gctx, win, wout, bias, mask = take(12)
+    own_x, own_c, xw, cw, nw, nwt, ctxt, proj, gctx, win, wout, bias, mask = take(13)
     perms = take(9)
     pack_ref, p0_ref, p1_ref, p2_ref, r1_ref, r2_ref, imid_ref, ibot_ref, itop_ref = perms
     send_strip, recv_strip = take(4), take(4)
@@ -314,11 +308,23 @@
         kind, first, width = PIECES[rnd][g]
         right = proj if kind == "in" else cw
 
+        order = ORDERS[rnd][g]
+        left = nwt if kind == "in" else ctxt
+
         def rows_of(zl, _):
             at = pl.multiple_of(zl * 512 + half * 256, 256)
-            value = dot(nwt[pl.ds(at, 256), :], right[:, first : first + width]).reshape(32, 8, width)
-            both = jnp.concatenate([value[:, :, :LANES], value[:, :, LANES:]], 1)
-            target[zl] = both.astype(BF).reshape(2, 4, 4, 16, LANES)
+            value = dot(left[pl.ds(at, 256), :], right[:, first : first + width]).reshape(32, 8, width)
+            both = jnp.concatenate([value[:, :, :LANES], value[:, :, LANES:]], 1).astype(BF)
+            both = both.reshape(2, 4, 4, 16, LANES)
+            for zh in range(2):
+                z = 2 * zh + zl
+                for end in range(2):
+                    part = both[zh, :, :, :, end * FIRST : (end + 1) * FIRST]
+                    if order.index("y") < order.index("x"):
+                        part = jnp.swapaxes(part, 0, 1)
+                    place = [end, slice(None), slice(None), slice(None)]
+                    place[1 + order.index("z")] = z
+                    target[tuple(place)] = part
             return 0
 
         lax.fori_loop(0, 2, rows_of, 0)
@@ -343,28 +349,9 @@
             mine[...] = (mine[...].astype(F32) + halves[rnd, g][...].astype(F32)).astype(BF)
             ring_start_group(rnd, g, 0)
 
-    def source(rnd, g, phase):
-        dims = ("zl", "zh", "x", "y")
-        for axis in ORDERS[rnd][g][:phase]:
-            dims = left_dims(dims, axis)
-        return (owns[rnd, g] if phase == 0 else middles[rnd, g, phase - 1]), dims
-
     def chunk(rnd, g, phase, step, half):
-        ref, dims = source(rnd, g, phase)
-        axis = ORDERS[rnd][g][phase]
-        t = (me[axis] + step + 4) % 4
-        end = pl.ds(half * FIRST, FIRST)
-        place = []
-        for dim in dims:
-            if dim == axis:
-                place.append(t)
-            elif axis == "z" and dim == "zl":
-                place.append(t % 2)
-            elif axis == "z" and dim == "zh":
-                place.append(t // 2)
-            else:
-                place.append(slice(None))
-        return ref.at[tuple(place) + (slice(None), end)]
+        ref = owns[rnd, g] if phase == 0 else middles[rnd, g, phase - 1]
+        return ref.at[half, (me[ORDERS[rnd][g][phase]] + step + 4) % 4]
 
     def ring(rnd, g, phase, number, src, step):
         return remote(
@@ -411,7 +398,7 @@
                 ).astype(BF)
                 start = half * FIRST
                 if phase < 2:
-                    middles[rnd, g, phase][..., start : start + FIRST] = value
+                    middles[rnd, g, phase][half] = value
                     continue
                 kind, first, _ = PIECES[rnd][g]
                 target = gi_out if kind == "in" else go_out
@@ -535,41 +522,40 @@
     late_windows(6)
     ring_end(0, 0)
     late_windows(7)
+    start_round(1)
     ring_relay(0, 1)
-    start_round(1)
+
+    def turn_context(n, _):
+        at = pl.ds(pl.multiple_of(n * 256, 256), 256)
+        ctxt[at, :] = gctx[:, at].T
+        return 0
+
+    lax.fori_loop(0, 4, turn_context, 0)
+    start_round(2)
+    own_products(1)
     ring_end(0, 1)
-    own_products(1)
-    ring_relay(0, 2)
     attended_step(1)
     attended_step(2)
     back_out = pack_back(2, xw_out)
     end_core(1)
-
-    def turn_context(n, _):
-        at = pl.ds(pl.multiple_of(n * 256, 256), 256)
-        nwt[at, :] = gctx[:, at].T
-        return 0
-
-    lax.fori_loop(0, 4, turn_context, 0)
-    start_round(2)
     own_products(2)
     gain = grad_step(1)
-    ring_relay(1, 0)
+    end_core(2)
+    ring_relay(0, 2)
     gain += grad_step(2)
     back_grad = pack_back(3, cw)
-    end_core(2)
+    ring_relay(1, 0)
     gain += grad_step(0)
     for n in range(8):
         gain_mine[0, n : n + 1, :] = gain[:, n * 128 : (n + 1) * 128]
     gain_copies = gain_start(0)
+    ring_relay(2, 0)
     ring_end(1, 0)
-    ring_relay(2, 0)
     attended_step(0)
-    ring_end(0, 2)
     gain_mine[1] = gain_finish(0, gain_copies)
     gain_copies = gain_start(1)
+    ring_end(2, 0)
     ring_relay(1, 1)
-    ring_end(2, 0)
     for copy in back_out:
         copy.wait()
     assemble(own_x, xw_out, recv_strip[2])
@@ -577,12 +563,12 @@
     store_out.start()
     gain_mine[2] = gain_finish(1, gain_copies)
     gain_copies = gain_start(2)
+    ring_relay(2, 1)
     ring_end(1, 1)
-    ring_relay(2, 1)
     gain_mine[3] = gain_finish(2, gain_copies)
     gain_copies = gain_start(3)
+    ring_end(2, 1)
     ring_relay(1, 2)
-    ring_end(2, 1)
     for copy in back_grad:
         copy.wait()
     assemble(own_c, cw, recv_strip[3])
@@ -590,6 +576,7 @@
     store_grad.start()
     ring_relay(2, 2)
     gg_out[...] = gain_finish(3, gain_copies)
+    ring_end(0, 2)
     ring_end(1, 2)
     ring_end(2, 2)
     store_out.wait()
@@ -602,20 +589,18 @@
     perms = [jnp.asarray(m, BF) for m in permutations()]
     wide = lambda rows, columns=D: pltpu.VMEM((rows, columns), BF)
     scratch = [wide(OWN) for _ in range(5)]
-    scratch += [wide(D, OWN), wide(OWN, 3 * D), wide(OWN), wide(D, 3 * D), wide(D)]
+    scratch += [wide(D, OWN), wide(D, OWN), wide(OWN, 3 * D), wide(OWN), wide(D, 3 * D), wide(D)]
     scratch += [pltpu.VMEM((16, WINT, WINT), F32), pltpu.VMEM((2, 2, WINT, WINT), F32)]
     scratch += [wide(*m.shape[1:]) for m in perms]
     scratch += [wide(STRIP) for _ in range(8)]
-    scratch += [pltpu.VMEM((2, 2, 4, 4, 16, LANES), BF) for _ in range(3 * len(GROUPS))]
+    scratch += [pltpu.VMEM((2, 4, 4, 4, 16, FIRST), BF) for _ in range(3 * len(GROUPS))]
     middles = []
     for r, g in GROUPS:
-        dims = ("zl", "zh", "x", "y")
         for phase in range(3):
-            dims = left_dims(dims, ORDERS[r][g][phase])
-            lead = tuple(SIZES[d] for d in dims)
+            lead = (4,) * (2 - phase)
             scratch += [pltpu.VMEM(lead + (16, FIRST), BF) for _ in range(8)]
             if phase < 2:
-                middles.append(pltpu.VMEM(lead + (16, LANES), BF))
+                middles.append(pltpu.VMEM((2,) + lead + (16, FIRST), BF))
     scratch += middles
     scratch += [pltpu.VMEM((4, 8, 128), F32), pltpu.VMEM((10, 8, 128), F32)]
     dma = pltpu.SemaphoreType.DMA

time: 135 us -> 136 us (level)
  Pallas kernels: 127 us -> 129 us
where the time goes in v3:
time: 136 us
  Pallas kernels  129 us (95%)
  local copies, waits for them, and re-layouts  6.67 us (5%)
    pallas_call x1, Pallas kernels, block(): pl.pallas_call(block_kernel, in_specs=[hbm, hbm, vm, hbm, hbm, hbm, vm] +...  129 us
    unnamed x10, local copies, waits for them, and re-layouts  5.41 us

profile of v3, /device:TPU:1, one launch (start us, length us, event | category | flops | bytes accessed | tf_op | source)
XLA Modules:
  0.0 135.9 jit_solution(17171318498566255117)
XLA Ops:
  0.6 128.6 %shard_map.191 = (bf16[864,1024]{1,0:T(8,128)(2,1)}, bf16[864,1024]{1,0:T(8,128)(2,1)}, bf16[8,3072]{1,0:T(8,128)(2,1)}, bf16[8,1024]{1,0:T(8,128)(2,1)}, f32[8,128]{1,0:T(8,128)}) custom-call(bf16[864,1024]{1,0:T(8,128)(2,1)} %bitcast.8, bf16[864,1024]{1,0:T(8,128)(2,1)} %bitcast.9, f32[1,1024]{1,0:T(1,128)} %bitcast.10, bf16[1024,3072]{1,0:T(8,128)(2,1)} %win_hbm.1, ...), custom_call_target="tpu_custom_call" | custom-call | tf_op jit(solution)/shard_map/pallas_call | solution.py:609
  129.3 1.3 dynamic_slice.3
  130.5 0.0 copy-start
  130.5 3.0 %copy.25 = bf16[2,18,24,1024]{3,2,1,0:T(8,128)(2,1)} copy(bf16[2,18,24,1024]{3,2,1,0:T(8,128)(2,1)} %bitcast.7) | data formatting | bytes 3538944
  133.5 0.0 copy-done
  133.5 0.0 copy-start.1
  133.5 0.0 copy-start.2
  133.5 1.2 copy.26
  134.7 0.0 copy-done.1
  134.7 0.6 copy.27
  135.3 0.0 copy-done.2
  135.3 0.6 copy.28
Async XLA Ops:
  130.5 3.0 %copy-start = (bf16[864,1024]{1,0:T(8,128)(2,1)S(1)}, bf16[864,1024]{1,0:T(8,128)(2,1)}, u32[]{:S(2)}) copy-start(bf16[864,1024]{1,0:T(8,128)(2,1)} %get-tuple-element.11) | copy-start | bytes 5308420
  133.5 1.2 copy-start.1
  133.5 1.8 %copy-start.2 = (bf16[8,1024]{1,0:T(8,128)(2,1)S(1)}, bf16[8,1024]{1,0:T(8,128)(2,1)}, u32[]{:S(2)}) copy-start(bf16[8,1024]{1,0:T(8,128)(2,1)} %get-tuple-element.23) | copy-start | bytes 49156

commit v4 on v3

--- a/solution.py
+++ b/solution.py
@@ -105,7 +105,7 @@
 def region_mask():
     region = np.array([a < 3 for l in range(2) for a in range(6) for b in range(12)])
     one = np.where(region[:, None] == region[None, :], 0.0, -1e9).astype(np.float32)
-    return np.concatenate([one, one], 0)
+    return np.concatenate([one] * 4, 1)
 
 
 def dg(a, b, dims):
@@ -133,14 +133,14 @@
         del scratch[:count]
         return out
 
-    own_x, own_c, xw, cw, nw, nwt, ctxt, proj, gctx, win, wout, bias, mask = take(13)
+    own_x, own_c, xw, cw, nw, nwt, proj, gctx, win, wout, raw, bias, mask = take(13)
     perms = take(9)
     pack_ref, p0_ref, p1_ref, p2_ref, r1_ref, r2_ref, imid_ref, ibot_ref, itop_ref = perms
-    send_strip, recv_strip = take(4), take(4)
+    send_strip, recv_strip = take(2) * 2, take(4)
     sends = {at: take(1)[0] for at in GROUPS}
     owns = {at: take(1)[0] for at in GROUPS}
     halves = {at: take(1)[0] for at in GROUPS}
-    landing = {(r, g, p): take(8) for r, g in GROUPS for p in range(3)}
+    landing = {(r, g, p): take(3 if p else 8) for r, g in GROUPS for p in range(3)}
     middles = {(r, g, p): take(1)[0] for r, g in GROUPS for p in range(2)}
     gain_mine, gain_land = take(2)
     load_sem, strip_send, strip_recv, core_send, core_recv = take(5)
@@ -166,13 +166,13 @@
         for n, (src, dst) in enumerate(
             (
                 (tok_hbm, own_x), (pack_hbm.at[core], pack_ref), (cot_hbm, own_c), (p0_hbm.at[core], p0_ref),
-                (win_hbm, win), (wout_hbm, wout), (hb_hbm, bias), (p1_hbm.at[core], p1_ref), (p2_hbm.at[core], p2_ref),
+                (hb_hbm, raw), (win_hbm, win), (wout_hbm, wout), (p1_hbm.at[core], p1_ref), (p2_hbm.at[core], p2_ref),
                 (r1_hbm.at[core], r1_ref), (r2_hbm.at[core], r2_ref), (imid_hbm.at[core], imid_ref),
                 (ibot_hbm.at[core], ibot_ref), (itop_hbm.at[core], itop_ref),
             )
         )
     ]
-    for load in loads:
+    for load in loads[:4]:
         load.start()
 
     barrier = pltpu.get_barrier_semaphore()
@@ -215,6 +215,8 @@
     strip_copies = []
     loads[0].wait()
     loads[1].wait()
+    for load in loads[4:7]:
+        load.start()
     for number, own in ((0, own_x), (1, own_c)):
         if number == 1:
             loads[2].wait()
@@ -267,53 +269,56 @@
 
         lax.fori_loop(0, 2, outer, 0)
 
+    head = lax.broadcasted_iota(jnp.int32, (WINT, 256), 1) // 64
     low_half = lax.broadcasted_iota(jnp.int32, (WINT, 128), 1) < 64
-    zero = jnp.zeros((WINT, 128), BF)
+    zero = jnp.zeros((WINT, 256), BF)
+
+    def stacked(a):
+        return jnp.concatenate([jnp.where(head == h, a, zero) for h in range(4)], 0)
+
+    def by_query(scores, a):
+        turned = scores.T
+        parts = []
+        for n in range(2):
+            both = dot(turned[n * PAIR : (n + 1) * PAIR], a[:, n * 128 : (n + 1) * 128])
+            parts.append(jnp.where(low_half, both[:WINT], both[WINT:]))
+        return jnp.concatenate(parts, 1)
 
     def unit(w, p, masked):
         rows = pl.ds(pl.multiple_of(w * WINT, 16), WINT)
-        at_q = pl.ds(pl.multiple_of(p * 128, 128), 128)
-        at_k = pl.ds(pl.multiple_of(1024 + p * 128, 128), 128)
-        at_v = pl.ds(pl.multiple_of(2048 + p * 128, 128), 128)
+        at_q = pl.ds(pl.multiple_of(p * 256, 256), 256)
+        at_k = pl.ds(pl.multiple_of(1024 + p * 256, 256), 256)
+        at_v = pl.ds(pl.multiple_of(2048 + p * 256, 256), 256)
         q, k, v, d = proj[rows, at_q], proj[rows, at_k], proj[rows, at_v], gctx[rows, at_q]
-        ks = jnp.concatenate([jnp.where(low_half, k, zero), jnp.where(low_half, zero, k)], 0)
-        vs = jnp.concatenate([jnp.where(low_half, v, zero), jnp.where(low_half, zero, v)], 0)
-        offset = bias[pl.ds(2 * p, 2)]
-        if masked is not None:
-            offset = offset + mask[masked]
-        st = dg(ks, q, NT).reshape(2, WINT, WINT) + offset
-        powers = jnp.exp(st - jnp.max(st, axis=1, keepdims=True))
-        weights = powers * (1.0 / jnp.sum(powers, axis=1, keepdims=True))
-        wb = weights.astype(BF).reshape(PAIR, WINT)
-        gctx[rows, at_q] = dg(wb, vs, TN).astype(BF)
-        dw = dg(vs, d, NT).reshape(2, WINT, WINT)
-        inner = jnp.sum(dw * weights, axis=1, keepdims=True)
-        ds = (weights * (dw - inner)).astype(BF).reshape(PAIR, WINT)
-        gv = dot(wb, d)
-        gk = dot(ds, q)
-        proj[rows, at_q] = (dg(ds, ks, TN) * 0.125).astype(BF)
-        proj[rows, at_k] = jnp.where(low_half, gk[:WINT], gk[WINT:]).astype(BF)
-        proj[rows, at_v] = jnp.where(low_half, gv[:WINT], gv[WINT:]).astype(BF)
-
-    def late_windows(p):
-        def two(t, _):
-            masked = jnp.where(t == 0, 1, 0)
-            unit(2 + 2 * t, p, masked)
-            unit(3 + 2 * t, p, masked)
-            return 0
-
-        lax.fori_loop(0, 2, two, 0)
+        qs, ds = stacked(q), stacked(d)
+        offset = bias[p]
+        if masked:
+            offset = offset + mask[...]
+        st = dg(k, qs, NT) + offset
+        powers = jnp.exp(st - jnp.max(st, axis=0, keepdims=True))
+        weights = powers * (1.0 / jnp.sum(powers, axis=0, keepdims=True))
+        wb = weights.astype(BF)
+        dw = dg(v, ds, NT)
+        inner = jnp.sum(dw * weights, axis=0, keepdims=True)
+        gs = (weights * (dw - inner)).astype(BF)
+        gctx[rows, at_q] = by_query(wb, v).astype(BF)
+        proj[rows, at_q] = (by_query(gs, k) * 0.125).astype(BF)
+        proj[rows, at_k] = dot(gs, qs).astype(BF)
+        proj[rows, at_v] = dot(wb, ds).astype(BF)
+
+    def late_windows(p, t):
+        unit(2 + 2 * t, p, t == 0)
+        unit(3 + 2 * t, p, t == 0)
 
     def products(rnd, g, half, target):
         kind, first, width = PIECES[rnd][g]
         right = proj if kind == "in" else cw
 
         order = ORDERS[rnd][g]
-        left = nwt if kind == "in" else ctxt
 
         def rows_of(zl, _):
             at = pl.multiple_of(zl * 512 + half * 256, 256)
-            value = dot(left[pl.ds(at, 256), :], right[:, first : first + width]).reshape(32, 8, width)
+            value = dot(nwt[pl.ds(at, 256), :], right[:, first : first + width]).reshape(32, 8, width)
             both = jnp.concatenate([value[:, :, :LANES], value[:, :, LANES:]], 1).astype(BF)
             both = both.reshape(2, 4, 4, 16, LANES)
             for zh in range(2):
@@ -365,47 +370,61 @@
     flying = {}
 
     def ring_start_group(rnd, g, phase):
+        if phase == 0:
+            flying[rnd, g] = {
+                0: ring(rnd, g, phase, 0, chunk(rnd, g, phase, 2, 0), 1),
+                3: ring(rnd, g, phase, 3, chunk(rnd, g, phase, 2, 1), -1),
+                1: ring(rnd, g, phase, 1, chunk(rnd, g, phase, 1, 1), 1),
+                4: ring(rnd, g, phase, 4, chunk(rnd, g, phase, -1, 0), -1),
+            }
+            return
         flying[rnd, g] = {
-            0: ring(rnd, g, phase, 0, chunk(rnd, g, phase, 2, 0), 1),
-            3: ring(rnd, g, phase, 3, chunk(rnd, g, phase, 2, 1), -1),
-            1: ring(rnd, g, phase, 1, chunk(rnd, g, phase, 1, 1), 1),
-            4: ring(rnd, g, phase, 4, chunk(rnd, g, phase, -1, 0), -1),
+            n: ring(rnd, g, phase, n, chunk(rnd, g, phase, n + 1, slice(None)), n + 1) for n in range(3)
         }
 
-    def ring_relay(rnd, phase):
+    def ring_relay(rnd):
         for g in range(len(ORDERS[rnd])):
-            land = landing[rnd, g, phase]
+            land = landing[rnd, g, 0]
             for number, step, half, slot in ((0, 1, 0, 6), (3, -1, 1, 7)):
                 flying[rnd, g][number].wait_recv()
                 land[slot][...] = (
-                    land[number][...].astype(F32) + chunk(rnd, g, phase, step, half)[...].astype(F32)
+                    land[number][...].astype(F32) + chunk(rnd, g, 0, step, half)[...].astype(F32)
                 ).astype(BF)
-                flying[rnd, g][number + 2] = ring(rnd, g, phase, number + 2, land[slot], step)
+                flying[rnd, g][number + 2] = ring(rnd, g, 0, number + 2, land[slot], step)
 
     def ring_end(rnd, phase):
         for g in range(len(ORDERS[rnd])):
             land = landing[rnd, g, phase]
             copies = flying[rnd, g]
-            for number in (1, 4, 2, 5):
+            if phase == 0:
+                for number in (1, 4, 2, 5):
+                    copies[number].wait()
+                copies[0].wait_send()
+                copies[3].wait_send()
+                for half, near, far in ((0, 4, 2), (1, 1, 5)):
+                    middles[rnd, g, phase][half] = (
+                        chunk(rnd, g, phase, 0, half)[...].astype(F32)
+                        + land[near][...].astype(F32)
+                        + land[far][...].astype(F32)
+                    ).astype(BF)
+                ring_start_group(rnd, g, 1)
+                continue
+            for number in range(3):
                 copies[number].wait()
-            copies[0].wait_send()
-            copies[3].wait_send()
-            for half, near, far in ((0, 4, 2), (1, 1, 5)):
-                value = (
-                    chunk(rnd, g, phase, 0, half)[...].astype(F32)
-                    + land[near][...].astype(F32)
-                    + land[far][...].astype(F32)
-                ).astype(BF)
-                start = half * FIRST
-                if phase < 2:
-                    middles[rnd, g, phase][half] = value
-                    continue
-                kind, first, _ = PIECES[rnd][g]
-                target = gi_out if kind == "in" else go_out
-                target[:, first + start : first + start + FIRST] = value[:8]
-                target[:, first + LANES + start : first + LANES + start + FIRST] = value[8:]
-            if phase < 2:
-                ring_start_group(rnd, g, phase + 1)
+            value = chunk(rnd, g, phase, 0, slice(None))[...].astype(F32)
+            for number in range(3):
+                value = value + land[number][...].astype(F32)
+            value = value.astype(BF)
+            if phase == 1:
+                middles[rnd, g, phase][...] = value
+                ring_start_group(rnd, g, 2)
+                continue
+            kind, first, _ = PIECES[rnd][g]
+            target = gi_out if kind == "in" else go_out
+            for half in range(2):
+                at = first + half * FIRST
+                target[:, at : at + FIRST] = value[half, :8]
+                target[:, at + LANES : at + LANES + FIRST] = value[half, 8:]
 
     def gain_start(stage):
         if stage == 0:
@@ -471,25 +490,30 @@
     loads[3].wait()
     gather_tokens(0)
     gather_cotangent(0)
-    for load in loads[4:]:
+    loads[4].wait()
+    mask[...] = jnp.where(lat == 3, 1.0, 0.0) * mask_ref[...]
+
+    def turn(p, _):
+        for h in range(4):
+            bias[p, :, h * WINT : (h + 1) * WINT] = raw[4 * p + h].T
+        return 0
+
+    lax.fori_loop(0, 4, turn, 0)
+    loads[5].wait()
+    project(0, PAIR)
+    loads[6].wait()
+    project_back(0, PAIR)
+    for load in loads[7:]:
+        load.start()
+
+    def early(p, _):
+        unit(0, p, False)
+        unit(1, p, False)
+        return 0
+
+    lax.fori_loop(0, 4, early, 0)
+    for load in loads[7:]:
         load.wait()
-    mask[0] = jnp.zeros((2, WINT, WINT), F32)
-    mask[1] = jnp.where(lat == 3, 1.0, 0.0) * mask_ref[...].reshape(2, WINT, WINT)
-
-    def turn(h, _):
-        bias[h] = bias[h].T
-        return 0
-
-    lax.fori_loop(0, 16, turn, 0)
-    project(0, PAIR)
-    project_back(0, PAIR)
-
-    def early(p, _):
-        unit(0, p, None)
-        unit(1, p, None)
-        return 0
-
-    lax.fori_loop(0, 8, early, 0)
     for copy in strip_copies[0]:
         copy.wait()
     gather_tokens(1)
@@ -509,31 +533,31 @@
     project_back(1, 2 * PAIR)
 
     def first_pairs(p, _):
-        late_windows(p)
+        late_windows(p, 0)
+        late_windows(p, 1)
         return 0
 
-    lax.fori_loop(0, 4, first_pairs, 0)
+    lax.fori_loop(0, 2, first_pairs, 0)
     start_round(0)
     own_products(0)
-    late_windows(4)
+    late_windows(2, 0)
     end_core(0)
-    late_windows(5)
-    ring_relay(0, 0)
-    late_windows(6)
+    late_windows(2, 1)
+    ring_relay(0)
+    late_windows(3, 0)
     ring_end(0, 0)
-    late_windows(7)
+    late_windows(3, 1)
     start_round(1)
-    ring_relay(0, 1)
+    own_products(1)
+    ring_end(0, 1)
 
     def turn_context(n, _):
         at = pl.ds(pl.multiple_of(n * 256, 256), 256)
-        ctxt[at, :] = gctx[:, at].T
+        nwt[at, :] = gctx[:, at].T
         return 0
 
     lax.fori_loop(0, 4, turn_context, 0)
     start_round(2)
-    own_products(1)
-    ring_end(0, 1)
     attended_step(1)
     attended_step(2)
     back_out = pack_back(2, xw_out)
@@ -541,43 +565,38 @@
     own_products(2)
     gain = grad_step(1)
     end_core(2)
-    ring_relay(0, 2)
     gain += grad_step(2)
     back_grad = pack_back(3, cw)
-    ring_relay(1, 0)
+    ring_end(0, 2)
+    ring_relay(1)
     gain += grad_step(0)
     for n in range(8):
         gain_mine[0, n : n + 1, :] = gain[:, n * 128 : (n + 1) * 128]
     gain_copies = gain_start(0)
-    ring_relay(2, 0)
+    ring_relay(2)
+    attended_step(0)
     ring_end(1, 0)
-    attended_step(0)
     gain_mine[1] = gain_finish(0, gain_copies)
     gain_copies = gain_start(1)
-    ring_end(2, 0)
-    ring_relay(1, 1)
     for copy in back_out:
         copy.wait()
     assemble(own_x, xw_out, recv_strip[2])
     store_out = pltpu.make_async_copy(own_x, out_hbm, load_sem.at[0])
     store_out.start()
+    ring_end(2, 0)
     gain_mine[2] = gain_finish(1, gain_copies)
     gain_copies = gain_start(2)
-    ring_relay(2, 1)
     ring_end(1, 1)
-    gain_mine[3] = gain_finish(2, gain_copies)
-    gain_copies = gain_start(3)
-    ring_end(2, 1)
-    ring_relay(1, 2)
     for copy in back_grad:
         copy.wait()
     assemble(own_c, cw, recv_strip[3])
     store_grad = pltpu.make_async_copy(own_c, gt_hbm, load_sem.at[1])
     store_grad.start()
-    ring_relay(2, 2)
+    ring_end(2, 1)
+    gain_mine[3] = gain_finish(2, gain_copies)
+    gain_copies = gain_start(3)
+    ring_end(1, 2)
     gg_out[...] = gain_finish(3, gain_copies)
-    ring_end(0, 2)
-    ring_end(1, 2)
     ring_end(2, 2)
     store_out.wait()
     store_grad.wait()
@@ -589,16 +608,19 @@
     perms = [jnp.asarray(m, BF) for m in permutations()]
     wide = lambda rows, columns=D: pltpu.VMEM((rows, columns), BF)
     scratch = [wide(OWN) for _ in range(5)]
-    scratch += [wide(D, OWN), wide(D, OWN), wide(OWN, 3 * D), wide(OWN), wide(D, 3 * D), wide(D)]
-    scratch += [pltpu.VMEM((16, WINT, WINT), F32), pltpu.VMEM((2, 2, WINT, WINT), F32)]
+    scratch += [wide(D, OWN), wide(OWN, 3 * D), wide(OWN), wide(D, 3 * D), wide(D)]
+    scratch += [pltpu.VMEM((16, WINT, WINT), F32), pltpu.VMEM((4, WINT, 4 * WINT), F32), pltpu.VMEM((WINT, 4 * WINT), F32)]
     scratch += [wide(*m.shape[1:]) for m in perms]
-    scratch += [wide(STRIP) for _ in range(8)]
+    scratch += [wide(STRIP) for _ in range(6)]
     scratch += [pltpu.VMEM((2, 4, 4, 4, 16, FIRST), BF) for _ in range(3 * len(GROUPS))]
     middles = []
     for r, g in GROUPS:
         for phase in range(3):
             lead = (4,) * (2 - phase)
-            scratch += [pltpu.VMEM(lead + (16, FIRST), BF) for _ in range(8)]
+            if phase == 0:
+                scratch += [pltpu.VMEM(lead + (16, FIRST), BF) for _ in range(8)]
+            else:
+                scratch += [pltpu.VMEM((2,) + lead + (16, FIRST), BF) for _ in range(3)]
             if phase < 2:
                 middles.append(pltpu.VMEM((2,) + lead + (16, FIRST), BF))
     scratch += middles

time: 136 us -> 120 us (0.88)
  Pallas kernels: 129 us -> 112 us
    pallas_call x1, Pallas kernels: 129 us -> 112 us  [block(): pl.pallas_call(block_kernel, in_specs=[hbm, hbm, vm, hbm, hbm, hbm, vm] +...]
where the time goes in v4:
time: 120 us
  Pallas kernels  112 us (93%)
  local copies, waits for them, and re-layouts  6.67 us (6%)
    pallas_call x1, Pallas kernels, block(): pl.pallas_call(block_kernel, in_specs=[hbm, hbm, vm, hbm, hbm, hbm, vm] +...  112 us
    unnamed x10, local copies, waits for them, and re-layouts  5.41 us

profile of v4, /device:TPU:1, one launch (start us, length us, event | category | flops | bytes accessed | tf_op | source)
XLA Modules:
  0.0 119.6 jit_solution(11354039190585921961)
XLA Ops:
  0.6 112.2 %shard_map.191 = (bf16[864,1024]{1,0:T(8,128)(2,1)}, bf16[864,1024]{1,0:T(8,128)(2,1)}, bf16[8,3072]{1,0:T(8,128)(2,1)}, bf16[8,1024]{1,0:T(8,128)(2,1)}, f32[8,128]{1,0:T(8,128)}) custom-call(bf16[864,1024]{1,0:T(8,128)(2,1)} %bitcast.6, bf16[864,1024]{1,0:T(8,128)(2,1)} %bitcast.7, f32[1,1024]{1,0:T(1,128)} %bitcast.10, bf16[1024,3072]{1,0:T(8,128)(2,1)} %win_hbm.1, ...), custom_call_target="tpu_custom_call" | custom-call | tf_op jit(solution)/shard_map/pallas_call | solution.py:631
  112.9 1.3 %dynamic_slice.3 = f32[8]{0:T(128)} dynamic-slice(f32[1024]{0:T(1024)} %bitcast.11, s32[]{:T(128)S(6)} %select_n.3), dynamic_slice_sizes={8} | dynamic-slice | bytes 68 | tf_op jit(solution)/shard_map/dynamic_slice | solution.py:659
  114.1 0.0 copy-start
  114.2 3.0 %copy.25 = bf16[2,18,24,1024]{3,2,1,0:T(8,128)(2,1)} copy(bf16[2,18,24,1024]{3,2,1,0:T(8,128)(2,1)} %bitcast.9) | data formatting | bytes 3538944
  117.1 0.0 copy-done
  117.1 0.0 copy-start.1
  117.1 0.0 copy-start.2
  117.1 1.2 %copy.26 = bf16[2,18,24,1024]{3,2,1,0:T(8,128)(2,1)} copy(bf16[2,18,24,1024]{3,2,1,0:T(8,128)(2,1)S(1)} %bitcast.8) | data formatting | bytes 3538944
  118.3 0.0 copy-done.1
  118.3 0.6 copy.27
  119.0 0.0 copy-done.2
  119.0 0.6 copy.28
Async XLA Ops:
  114.1 3.0 %copy-start = (bf16[864,1024]{1,0:T(8,128)(2,1)S(1)}, bf16[864,1024]{1,0:T(8,128)(2,1)}, u32[]{:S(2)}) copy-start(bf16[864,1024]{1,0:T(8,128)(2,1)} %get-tuple-element.11) | copy-start | bytes 5308420
  117.1 1.2 %copy-start.1 = (bf16[8,3072]{1,0:T(8,128)(2,1)S(1)}, bf16[8,3072]{1,0:T(8,128)(2,1)}, u32[]{:S(2)}) copy-start(bf16[8,3072]{1,0:T(8,128)(2,1)} %get-tuple-element.22) | copy-start | bytes 147460
  117.1 1.8 %copy-start.2 = (bf16[8,1024]{1,0:T(8,128)(2,1)S(1)}, bf16[8,1024]{1,0:T(8,128)(2,1)}, u32[]{:S(2)}) copy-start(bf16[8,1024]{1,0:T(8,128)(2,1)} %get-tuple-element.23) | copy-start | bytes 49156

commit v5 on v4

--- a/solution.py
+++ b/solution.py
@@ -540,16 +540,12 @@
     lax.fori_loop(0, 2, first_pairs, 0)
     start_round(0)
     own_products(0)
-    late_windows(2, 0)
+    for p in (2, 3):
+        for t in range(2):
+            late_windows(p, t)
+    start_round(1)
     end_core(0)
-    late_windows(2, 1)
-    ring_relay(0)
-    late_windows(3, 0)
-    ring_end(0, 0)
-    late_windows(3, 1)
-    start_round(1)
     own_products(1)
-    ring_end(0, 1)
 
     def turn_context(n, _):
         at = pl.ds(pl.multiple_of(n * 256, 256), 256)
@@ -561,19 +557,21 @@
     attended_step(1)
     attended_step(2)
     back_out = pack_back(2, xw_out)
+    ring_relay(0)
     end_core(1)
     own_products(2)
     gain = grad_step(1)
     end_core(2)
+    ring_end(0, 0)
     gain += grad_step(2)
     back_grad = pack_back(3, cw)
-    ring_end(0, 2)
     ring_relay(1)
     gain += grad_step(0)
     for n in range(8):
         gain_mine[0, n : n + 1, :] = gain[:, n * 128 : (n + 1) * 128]
     gain_copies = gain_start(0)
     ring_relay(2)
+    ring_end(0, 1)
     attended_step(0)
     ring_end(1, 0)
     gain_mine[1] = gain_finish(0, gain_copies)
@@ -595,9 +593,10 @@
     ring_end(2, 1)
     gain_mine[3] = gain_finish(2, gain_copies)
     gain_copies = gain_start(3)
+    ring_end(0, 2)
     ring_end(1, 2)
+    ring_end(2, 2)
     gg_out[...] = gain_finish(3, gain_copies)
-    ring_end(2, 2)
     store_out.wait()
     store_grad.wait()
 
@@ -649,14 +648,42 @@
     )
 
 
+def finish_kernel(out_ref, gt_ref, gi_ref, go_ref, gg_ref, out_final, gt_final, gi_final, go_final, gain_final):
+    out_final[...] = out_ref[...]
+    gt_final[...] = gt_ref[...]
+    gi_final[...] = gi_ref[...]
+    go_final[...] = go_ref[...]
+    at = (lax.axis_index("lat") * 32 + lax.axis_index("lon")) * 8
+    place = lax.broadcasted_iota(jnp.int32, (8, 128), 0) * 128 + lax.broadcasted_iota(jnp.int32, (8, 128), 1)
+    for n in range(8):
+        gain_final[n] = jnp.sum(jnp.where(place == at + n, gg_ref[...], 0.0))
+
+
+def finish(*results):
+    vm = pl.BlockSpec(memory_space=pltpu.VMEM)
+    rows = pl.BlockSpec((PAIR, D), lambda i: (i, 0))
+    return pl.pallas_call(
+        finish_kernel,
+        grid=(3,),
+        in_specs=[rows, rows, vm, vm, vm],
+        out_specs=[rows, rows, vm, vm, pl.BlockSpec(memory_space=pltpu.SMEM)],
+        out_shape=[
+            jax.ShapeDtypeStruct((OWN, D), BF),
+            jax.ShapeDtypeStruct((OWN, D), BF),
+            jax.ShapeDtypeStruct((8, 3 * D), BF),
+            jax.ShapeDtypeStruct((8, D), BF),
+            jax.ShapeDtypeStruct((8,), F32),
+        ],
+    )(*results)
+
+
 def local(tokens, norm_gain, attention_in, attention_out, head_bias, cotangent):
     shape = tokens.shape
-    lat = lax.axis_index("lat")
-    lon = lax.axis_index("lon")
-    out, gt, gi, go, gains = block(
-        tokens.reshape(OWN, D), cotangent.reshape(OWN, D), norm_gain, attention_in, attention_out, head_bias
+    out, gt, gi, go, gain = finish(
+        *block(
+            tokens.reshape(OWN, D), cotangent.reshape(OWN, D), norm_gain, attention_in, attention_out, head_bias
+        )
     )
-    gain = lax.dynamic_slice(gains.reshape(1024), ((lat * 32 + lon) * 8,), (8,))
     return out.reshape(shape), gt.reshape(shape), gi, go, gain
 
 

time: 120 us -> 111 us (0.925)
  local copies, waits for them, and re-layouts: 6.67 us -> 0 us
  Pallas kernels: 112 us -> 110 us
    pallas_call x1, Pallas kernels: 112 us -> 106 us  [block(): pl.pallas_call(block_kernel, in_specs=[hbm, hbm, vm, hbm, hbm, hbm, vm] +...]
    unnamed x10 -> x0, local copies, waits for them, and re-layouts: 5.41 us -> none
    pallas_call x0 -> x1, Pallas kernels: none -> 4.59 us  [finish(): pl.pallas_call(finish_kernel, grid=(3,), in_specs=[rows, rows, vm, vm, vm...]
    dynamic_slice x1 -> x0, local copies, waits for them, and re-layouts: 1.26 us -> none  [local(): gain = lax.dynamic_slice(gains.reshape(1024), ((lat * 32 + lon) * 8,), (8,))]
where the time goes in v5:
time: 111 us
  Pallas kernels  110 us (99%)
    pallas_call x1, Pallas kernels, block(): pl.pallas_call(block_kernel, in_specs=[hbm, hbm, vm, hbm, hbm, hbm, vm] +...  106 us
    pallas_call x1, Pallas kernels, finish(): pl.pallas_call(finish_kernel, grid=(3,), in_specs=[rows, rows, vm, vm, vm...  4.59 us

profile of v5, /device:TPU:1, one launch (start us, length us, event | category | flops | bytes accessed | tf_op | source)
XLA Modules:
  0.0 111.2 jit_solution(8327343900872571367)
XLA Ops:
  0.6 105.8 %shard_map.191 = (bf16[864,1024]{1,0:T(8,128)(2,1)}, bf16[864,1024]{1,0:T(8,128)(2,1)}, bf16[8,3072]{1,0:T(8,128)(2,1)}, bf16[8,1024]{1,0:T(8,128)(2,1)}, f32[8,128]{1,0:T(8,128)}) custom-call(bf16[864,1024]{1,0:T(8,128)(2,1)} %bitcast.5, bf16[864,1024]{1,0:T(8,128)(2,1)} %bitcast.6, f32[1,1024]{1,0:T(1,128)} %bitcast.7, bf16[1024,3072]{1,0:T(8,128)(2,1)} %win_hbm.1, ...), custom_call_target="tpu_custom_call" | custom-call | tf_op jit(solution)/shard_map/pallas_call | solution.py:630
  106.4 4.6 %shard_map.192 = (bf16[864,1024]{1,0:T(8,128)(2,1)}, bf16[864,1024]{1,0:T(8,128)(2,1)}, bf16[8,3072]{1,0:T(8,128)(2,1)}, bf16[8,1024]{1,0:T(8,128)(2,1)}, f32[8]{0:T(128)}) custom-call(bf16[864,1024]{1,0:T(8,128)(2,1)} %get-tuple-element.15.out_ref, bf16[864,1024]{1,0:T(8,128)(2,1)} %get-tuple-element.16.gt_ref, bf16[8,3072]{1,0:T(8,128)(2,1)} %get-tuple-element.17.gi_ref, ...), custom_call_target="tpu_custom_call" | custom-call | tf_op jit(solution)/shard_map/pallas_call | solution.py:665

commit v6 on v5

--- a/solution.py
+++ b/solution.py
@@ -362,8 +362,8 @@
         return remote(
             src,
             landing[rnd, g, phase][number],
-            ring_send.at[rnd, g, phase, number],
-            ring_recv.at[rnd, g, phase, number],
+            ring_send.at[GROUPS.index((rnd, g)), (0, 6, 9)[phase] + number],
+            ring_recv.at[GROUPS.index((rnd, g)), (0, 6, 9)[phase] + number],
             device(ORDERS[rnd][g][phase], step),
         )
 
@@ -554,43 +554,43 @@
 
     lax.fori_loop(0, 4, turn_context, 0)
     start_round(2)
+    own_products(2)
+    end_core(1)
+    ring_relay(0)
     attended_step(1)
     attended_step(2)
     back_out = pack_back(2, xw_out)
-    ring_relay(0)
-    end_core(1)
-    own_products(2)
+    end_core(2)
     gain = grad_step(1)
-    end_core(2)
+    ring_relay(1)
     ring_end(0, 0)
     gain += grad_step(2)
     back_grad = pack_back(3, cw)
-    ring_relay(1)
+    ring_relay(2)
+    ring_end(1, 0)
     gain += grad_step(0)
     for n in range(8):
         gain_mine[0, n : n + 1, :] = gain[:, n * 128 : (n + 1) * 128]
     gain_copies = gain_start(0)
-    ring_relay(2)
     ring_end(0, 1)
+    ring_end(2, 0)
     attended_step(0)
-    ring_end(1, 0)
     gain_mine[1] = gain_finish(0, gain_copies)
     gain_copies = gain_start(1)
+    ring_end(1, 1)
     for copy in back_out:
         copy.wait()
     assemble(own_x, xw_out, recv_strip[2])
     store_out = pltpu.make_async_copy(own_x, out_hbm, load_sem.at[0])
     store_out.start()
-    ring_end(2, 0)
     gain_mine[2] = gain_finish(1, gain_copies)
     gain_copies = gain_start(2)
-    ring_end(1, 1)
+    ring_end(2, 1)
     for copy in back_grad:
         copy.wait()
     assemble(own_c, cw, recv_strip[3])
     store_grad = pltpu.make_async_copy(own_c, gt_hbm, load_sem.at[1])
     store_grad.start()
-    ring_end(2, 1)
     gain_mine[3] = gain_finish(2, gain_copies)
     gain_copies = gain_start(3)
     ring_end(0, 2)
@@ -626,7 +626,7 @@
     scratch += [pltpu.VMEM((4, 8, 128), F32), pltpu.VMEM((10, 8, 128), F32)]
     dma = pltpu.SemaphoreType.DMA
     scratch += [dma((14,)), dma((4, 5)), dma((4, 5)), dma((3, 3)), dma((3, 3))]
-    scratch += [dma((3, 3, 3, 6)), dma((3, 3, 3, 6)), dma((10,)), dma((10,))]
+    scratch += [dma((len(GROUPS), 12)), dma((len(GROUPS), 12)), dma((10,)), dma((10,))]
     return pl.pallas_call(
         block_kernel,
         in_specs=[hbm, hbm, vm, hbm, hbm, hbm, vm] + [hbm] * 9,

time: 111 us -> 113 us (1.018)
  Pallas kernels: 110 us -> 112 us
    pallas_call x1, Pallas kernels: 106 us -> 107 us  [block(): pl.pallas_call(block_kernel, in_specs=[hbm, hbm, vm, hbm, hbm, hbm, vm] +...]
where the time goes in v6:
time: 113 us; the launch traced here: 112 us
  Pallas kernels  112 us (99%)
    pallas_call x1, Pallas kernels, block(): pl.pallas_call(block_kernel, in_specs=[hbm, hbm, vm, hbm, hbm, hbm, vm] +...  107 us
    pallas_call x1, Pallas kernels, finish(): pl.pallas_call(finish_kernel, grid=(3,), in_specs=[rows, rows, vm, vm, vm...  4.59 us

profile of v6, /device:TPU:1, one launch (start us, length us, event | category | flops | bytes accessed | tf_op | source)
XLA Modules:
  0.0 112.4 jit_solution(17386917048168583061)
XLA Ops:
  0.6 107.0 %shard_map.191 = (bf16[864,1024]{1,0:T(8,128)(2,1)}, bf16[864,1024]{1,0:T(8,128)(2,1)}, bf16[8,3072]{1,0:T(8,128)(2,1)}, bf16[8,1024]{1,0:T(8,128)(2,1)}, f32[8,128]{1,0:T(8,128)}) custom-call(bf16[864,1024]{1,0:T(8,128)(2,1)} %bitcast.5, bf16[864,1024]{1,0:T(8,128)(2,1)} %bitcast.6, f32[1,1024]{1,0:T(1,128)} %bitcast.7, bf16[1024,3072]{1,0:T(8,128)(2,1)} %win_hbm.1, ...), custom_call_target="tpu_custom_call" | custom-call | tf_op jit(solution)/shard_map/pallas_call | solution.py:630
  107.7 4.6 %shard_map.192 = (bf16[864,1024]{1,0:T(8,128)(2,1)}, bf16[864,1024]{1,0:T(8,128)(2,1)}, bf16[8,3072]{1,0:T(8,128)(2,1)}, bf16[8,1024]{1,0:T(8,128)(2,1)}, f32[8]{0:T(128)}) custom-call(bf16[864,1024]{1,0:T(8,128)(2,1)} %get-tuple-element.15.out_ref, bf16[864,1024]{1,0:T(8,128)(2,1)} %get-tuple-element.16.gt_ref, bf16[8,3072]{1,0:T(8,128)(2,1)} %get-tuple-element.17.gi_ref, ...), custom_call_target="tpu_custom_call" | custom-call | tf_op jit(solution)/shard_map/pallas_call | solution.py:665

commit v7 on v5

--- a/solution.py
+++ b/solution.py
@@ -362,8 +362,8 @@
         return remote(
             src,
             landing[rnd, g, phase][number],
-            ring_send.at[rnd, g, phase, number],
-            ring_recv.at[rnd, g, phase, number],
+            ring_send.at[GROUPS.index((rnd, g)), (0, 6, 9)[phase] + number],
+            ring_recv.at[GROUPS.index((rnd, g)), (0, 6, 9)[phase] + number],
             device(ORDERS[rnd][g][phase], step),
         )
 
@@ -540,11 +540,12 @@
     lax.fori_loop(0, 2, first_pairs, 0)
     start_round(0)
     own_products(0)
-    for p in (2, 3):
-        for t in range(2):
-            late_windows(p, t)
+    late_windows(2, 0)
+    late_windows(2, 1)
+    end_core(0)
+    late_windows(3, 0)
+    late_windows(3, 1)
     start_round(1)
-    end_core(0)
     own_products(1)
 
     def turn_context(n, _):
@@ -626,7 +627,7 @@
     scratch += [pltpu.VMEM((4, 8, 128), F32), pltpu.VMEM((10, 8, 128), F32)]
     dma = pltpu.SemaphoreType.DMA
     scratch += [dma((14,)), dma((4, 5)), dma((4, 5)), dma((3, 3)), dma((3, 3))]
-    scratch += [dma((3, 3, 3, 6)), dma((3, 3, 3, 6)), dma((10,)), dma((10,))]
+    scratch += [dma((len(GROUPS), 12)), dma((len(GROUPS), 12)), dma((10,)), dma((10,))]
     return pl.pallas_call(
         block_kernel,
         in_specs=[hbm, hbm, vm, hbm, hbm, hbm, vm] + [hbm] * 9,
@@ -661,10 +662,10 @@
 
 def finish(*results):
     vm = pl.BlockSpec(memory_space=pltpu.VMEM)
-    rows = pl.BlockSpec((PAIR, D), lambda i: (i, 0))
+    rows = pl.BlockSpec((432, D), lambda i: (i, 0))
     return pl.pallas_call(
         finish_kernel,
-        grid=(3,),
+        grid=(2,),
         in_specs=[rows, rows, vm, vm, vm],
         out_specs=[rows, rows, vm, vm, pl.BlockSpec(memory_space=pltpu.SMEM)],
         out_shape=[
@@ -674,6 +675,7 @@
             jax.ShapeDtypeStruct((8, D), BF),
             jax.ShapeDtypeStruct((8,), F32),
         ],
+        compiler_params=pltpu.CompilerParams(vmem_limit_bytes=32 * 2**20),
     )(*results)
 
 

time: 111 us -> 113 us (1.018)
  local copies, waits for them, and re-layouts: 0 us -> 5.14 us
  Pallas kernels: 110 us -> 107 us
    unnamed x0 -> x10, local copies, waits for them, and re-layouts: none -> 5.14 us
    pallas_call x1, Pallas kernels: 4.59 us -> 1.91 us  [finish(): pl.pallas_call(finish_kernel, grid=(2,), in_specs=[rows, rows, vm, vm, vm...]
where the time goes in v7:
time: 113 us
  Pallas kernels  107 us (95%)
  local copies, waits for them, and re-layouts  5.14 us (5%)
    pallas_call x1, Pallas kernels, block(): pl.pallas_call(block_kernel, in_specs=[hbm, hbm, vm, hbm, hbm, hbm, vm] +...  105 us
    unnamed x10, local copies, waits for them, and re-layouts  5.14 us

profile of v7, /device:TPU:1, one launch (start us, length us, event | category | flops | bytes accessed | tf_op | source)
XLA Modules:
  0.0 112.6 jit_solution(12822813113166574954)
XLA Ops:
  0.6 104.8 %shard_map.191 = (bf16[864,1024]{1,0:T(8,128)(2,1)}, bf16[864,1024]{1,0:T(8,128)(2,1)}, bf16[8,3072]{1,0:T(8,128)(2,1)}, bf16[8,1024]{1,0:T(8,128)(2,1)}, f32[8,128]{1,0:T(8,128)}) custom-call(bf16[864,1024]{1,0:T(8,128)(2,1)} %bitcast.5, bf16[864,1024]{1,0:T(8,128)(2,1)} %bitcast.6, f32[1,1024]{1,0:T(1,128)} %bitcast.7, bf16[1024,3072]{1,0:T(8,128)(2,1)} %win_hbm.1, ...), custom_call_target="tpu_custom_call" | custom-call | tf_op jit(solution)/shard_map/pallas_call | solution.py:631
  105.4 0.0 copy-start
  105.4 1.5 %copy-done = bf16[864,1024]{1,0:T(8,128)(2,1)S(1)} copy-done((bf16[864,1024]{1,0:T(8,128)(2,1)S(1)}, bf16[864,1024]{1,0:T(8,128)(2,1)}, u32[]{:S(2)}) %copy-start) | copy-done | bytes 1769496
  106.9 0.0 copy-start.1
  106.9 1.5 %copy-done.1 = bf16[864,1024]{1,0:T(8,128)(2,1)S(1)} copy-done((bf16[864,1024]{1,0:T(8,128)(2,1)S(1)}, bf16[864,1024]{1,0:T(8,128)(2,1)}, u32[]{:S(2)}) %copy-start.1) | copy-done | bytes 1769496
  108.4 0.0 copy-start.2
  108.4 0.8 copy-done.2
  109.2 0.0 copy-start.3
  109.2 0.7 copy-done.3
  109.9 0.0 copy-start.4
  109.9 0.7 copy-done.4
  110.6 1.9 %shard_map.192 = (bf16[864,1024]{1,0:T(8,128)(2,1)}, bf16[864,1024]{1,0:T(8,128)(2,1)}, bf16[8,3072]{1,0:T(8,128)(2,1)}, bf16[8,1024]{1,0:T(8,128)(2,1)}, f32[8]{0:T(128)}) custom-call(bf16[864,1024]{1,0:T(8,128)(2,1)S(1)} %copy-done, bf16[864,1024]{1,0:T(8,128)(2,1)S(1)} %copy-done.1, bf16[8,3072]{1,0:T(8,128)(2,1)S(1)} %copy-done.2, ...), custom_call_target="tpu_custom_call" | custom-call | tf_op jit(solution)/shard_map/pallas_call | solution.py:666
Async XLA Ops:
  105.4 1.5 %copy-start = (bf16[864,1024]{1,0:T(8,128)(2,1)S(1)}, bf16[864,1024]{1,0:T(8,128)(2,1)}, u32[]{:S(2)}) copy-start(bf16[864,1024]{1,0:T(8,128)(2,1)} %get-tuple-element.15.out_ref) | copy-start | bytes 5308420
  106.9 1.5 %copy-start.1 = (bf16[864,1024]{1,0:T(8,128)(2,1)S(1)}, bf16[864,1024]{1,0:T(8,128)(2,1)}, u32[]{:S(2)}) copy-start(bf16[864,1024]{1,0:T(8,128)(2,1)} %get-tuple-element.16.gt_ref) | copy-start | bytes 5308420
  108.4 0.8 copy-start.2
  109.2 0.7 copy-start.3
  109.9 0.7 copy-start.4
